TPU v7x, 256 devices: a whole 4x4x8 slice. The times are simulated.
256 devices in a mesh: dp: 32 (over y, x, core), mp: 8 (over z).
Axes of the slice: x: 4, y: 4, z: 8, core: 2. Of those that a mesh axis runs over, the one named last changes fastest.
Arguments:
- patches: bfloat16 [4096, 3200], P('dp'), may hold values from -6 to 6
- upstream: bfloat16 [4096, 3200], P('dp'), may hold values from -6 to 6
- norm_gain: float32 [3200], replicated, may hold values from 0.25 to 1.75
- layer_scale: float32 [3200], replicated, may hold values from 0.3 to 1.5
- w_in: bfloat16 [3200, 6400], P('dp', 'mp'), may hold values from -0.109375 to 0.109375
- w_out: bfloat16 [6400, 3200], P('mp', 'dp'), may hold values from -0.078125 to 0.078125
- slot_block: int32 [64], P('dp'), may hold values from -1 to 255, as said below
Outputs:
- vision_tokens: bfloat16 [4096, 4, 3200], P('dp', None, 'mp')
- grad_patches: bfloat16 [4096, 3200], P('dp', 'mp')
- grad_w_in: float32 [3200, 6400], P('dp', 'mp')
- grad_w_out: float32 [6400, 3200], P('mp', 'dp')
Inputs may be any that keep to these rules, and one draw needn't show every extreme that they name: `slot_block`: every used block value is different. The used slots of one dp index send their tiles to different dp indices (block // 8), so one dp index receives at most one tile from each dp index and at most 2 tiles in all.
All inputs are finite; a program needn't handle non-finite values.
Results may differ from a plain program's by a relative error of at most 0.02.
Values may be sent and summed in bfloat16 or wider, within the bound.
A program may use at most 128 MiB of HBM per device.

v0:
```python
import jax
import jax.numpy as jnp
from jax import lax
from jax.sharding import PartitionSpec as P

BLK = 8


def gelu_terms(values):
    cumul = 0.5 * (1.0 + jax.scipy.special.erf(values * 0.7071067811865476))
    density = jnp.exp(-0.5 * values * values) * 0.3989422804014327
    return (cumul, density)


def columns(array, count, axis):
    return lax.dynamic_slice_in_dim(array, lax.axis_index("mp") * count, count, axis)


def shards(patches, upstream, norm_gain, layer_scale, w_in, w_out, slot_block):
    total_rows, width = patches.shape
    slots = slot_block.shape[0]
    tile_rows = total_rows // slots
    image_tok = tile_rows // 4
    share = width // lax.axis_size("mp")
    full_in, full_out = (
        lax.all_gather(w_in, "dp", axis=0, tiled=True),
        lax.all_gather(w_out, "dp", axis=1, tiled=True),
    )
    inputs = patches.astype(jnp.float32)
    root_mean = jnp.sqrt(jnp.mean(inputs * inputs, axis=-1, keepdims=True) + 1e-06)
    unit_rows = inputs / root_mean
    normed = (unit_rows * norm_gain).astype(jnp.bfloat16)
    hidden_in = jnp.dot(normed, full_in, preferred_element_type=jnp.float32)
    cumul, density = gelu_terms(hidden_in)
    hidden_out = (hidden_in * cumul).astype(jnp.bfloat16)
    mixed_mine = (
        lax.psum_scatter(
            lax.dot_general(
                full_out, hidden_out, (((0,), (1,)), ((), ())), preferred_element_type=jnp.float32
            ).astype(jnp.bfloat16),
            "mp",
            scatter_dimension=0,
            tiled=True,
        )
        .astype(jnp.float32)
        .T
    )
    scale_mine = columns(layer_scale, share, 0)
    result = (columns(inputs, share, 1) + scale_mine * mixed_mine).astype(jnp.bfloat16)
    shuffled = (
        result.reshape(slots, 2, image_tok, 2, share)
        .transpose(0, 2, 1, 3, 4)
        .reshape(slots, image_tok, 4, share)
    )
    owner = lax.axis_index("dp")
    arrived, arrived_blocks = (
        lax.all_gather(shuffled, "dp", axis=0, tiled=True),
        lax.all_gather(slot_block, "dp", axis=0, tiled=True),
    )
    local_block = arrived_blocks - owner * BLK
    placing = (local_block[None, :] == jnp.arange(BLK, dtype=jnp.int32)[:, None]).astype(
        jnp.bfloat16
    )
    placed = jnp.einsum("bq,qtuc->btuc", placing, arrived, preferred_element_type=jnp.float32)
    vision_tokens = placed.astype(jnp.bfloat16).reshape(BLK * image_tok, 4, share)
    live_row = jnp.repeat((slot_block >= 0).astype(jnp.float32), tile_rows)[:, None]
    live = upstream.astype(jnp.float32) * live_row
    grad_mixed = (live * layer_scale).astype(jnp.bfloat16)
    grad_hidden = lax.dot_general(
        grad_mixed, full_out, (((1,), (1,)), ((), ())), preferred_element_type=jnp.float32
    )
    grad_in = (grad_hidden * (cumul + hidden_in * density)).astype(jnp.bfloat16)
    part_in = lax.dot_general(
        normed, grad_in, (((0,), (0,)), ((), ())), preferred_element_type=jnp.float32
    )
    part_out = lax.dot_general(
        hidden_out, grad_mixed, (((0,), (0,)), ((), ())), preferred_element_type=jnp.float32
    )
    grad_w_in, grad_w_out = (
        lax.psum_scatter(
            part_in.astype(jnp.bfloat16), "dp", scatter_dimension=0, tiled=True
        ).astype(jnp.float32),
        lax.psum_scatter(
            part_out.astype(jnp.bfloat16), "dp", scatter_dimension=1, tiled=True
        ).astype(jnp.float32),
    )
    partial_normed = lax.dot_general(
        grad_in, full_in, (((1,), (1,)), ((), ())), preferred_element_type=jnp.float32
    )
    grad_normed = lax.psum(partial_normed.astype(jnp.bfloat16), "mp").astype(jnp.float32)
    scaled = norm_gain * grad_normed
    center = jnp.mean(scaled * unit_rows, axis=-1, keepdims=True)
    whole = live + (scaled - unit_rows * center) / root_mean
    grad_patches = columns(whole, share, 1).astype(jnp.bfloat16)
    return (vision_tokens, grad_patches, grad_w_in, grad_w_out)


def solution(mesh):
    return jax.shard_map(
        shards,
        mesh=mesh,
        in_specs=(P("dp", None), P("dp", None), P(), P(), P("dp", "mp"), P("mp", "dp"), P("dp")),
        out_specs=(P("dp", None, "mp"), P("dp", "mp"), P("dp", "mp"), P("mp", "dp")),
        check_vma=False,
    )
```

profile of v0, /device:TPU:1, one launch (start us, length us, event | category | flops | bytes accessed | tf_op | source)
XLA Modules:
  0.0 356.4 jit_solution(14304944772353284159)
XLA Ops:
  7.2 0.0 all-gather.8.cloned.1.call-start
  7.2 0.7 all-gather.8.cloned.1.call-update
  7.9 0.0 all-gather.10.cloned.1.call-start
  7.9 0.7 all-gather.10.cloned.1.call-update
  8.6 0.0 reduce-scatter.8.cloned.1.call-start
  8.7 1.4 multiply_reduce_fusion.1
  10.1 0.0 copy-start
  10.1 0.0 copy-start.3
  10.1 58.3 %all-gather.8.cloned.1.call-done = bf16[32,100,800]{2,1,0:T(8,128)(2,1)} async-done(((bf16[1,100,800]{2,1,0:T(8,128)(2,1)}), bf16[32,100,800]{2,1,0:T(8,128)(2,1)}) %all-gather.8.cloned.1.call-update) | async-done | bytes 5120016 | tf_op jit(solution)/shard_map/all_gather | solution.py:26
  68.4 8.4 %reshape.47 = bf16[3200,800]{1,0:T(8,128)(2,1)} reshape(bf16[32,100,800]{2,1,0:T(8,128)(2,1)} %all-gather.8.cloned.1.call-done) | data formatting | bytes 10240000
  76.8 4.9 %fusion.13 = f32[128,800]{0,1:T(8,128)S(1)} fusion(bf16[3200,800]{1,0:T(8,128)(2,1)} %reshape.47, f32[3200]{0:T(1024)S(1)} %copy-done.3, f32[128]{0:T(128)S(1)} %add_sqrt_fusion, bf16[128,3200]{1,0:T(8,128)(2,1)S(1)} %copy-done), kind=kOutput, calls=%fused_computation.24 | convolution fusion | flops 656998400 | bytes 6362112 | tf_op jit(solution)/shard_map/dot_general | solution.py:33
  81.7 42.0 %all-gather.10.cloned.1.call-done = bf16[32,100,800]{2,1,0:T(8,128)(2,1)} async-done(((bf16[1,100,800]{2,1,0:T(8,128)(2,1)}), bf16[32,100,800]{2,1,0:T(8,128)(2,1)}) %all-gather.10.cloned.1.call-update) | async-done | bytes 5120016 | tf_op jit(solution)/shard_map/all_gather | solution.py:27
  123.7 8.4 %reshape.48 = bf16[3200,800]{1,0:T(8,128)(2,1)} reshape(bf16[32,100,800]{2,1,0:T(8,128)(2,1)} %all-gather.10.cloned.1.call-done) | data formatting | bytes 10240000
  132.1 4.4 %fusion.2 = bf16[3200,128]{0,1:T(8,128)(2,1)S(1)} fusion(bf16[3200,800]{1,0:T(8,128)(2,1)} %reshape.48, f32[128,800]{0,1:T(8,128)S(1)} %fusion.13), kind=kOutput, calls=%fused_computation.4 | convolution fusion | flops 656281600 | bytes 6348800 | tf_op jit(solution)/shard_map/dot_general | solution.py:38
  136.6 0.0 copy-start.7
  136.6 0.0 copy-start.1
  136.6 0.0 copy-start.2
  136.6 1.3 copy.35
  137.9 0.0 reduce-scatter.8.cloned.1.call-update
  137.9 0.0 all-reduce.8.cloned.1.call-start
  138.0 0.1 broadcast_in_dim.2
  138.1 0.1 mul.114
  138.2 4.9 %fusion.8 = bf16[128,800]{0,1:T(8,128)(2,1)S(1)} fusion(bf16[3200,800]{1,0:T(8,128)(2,1)} %reshape.48, f32[128,800]{0,1:T(8,128)S(1)} %fusion.13, f32[3200]{0:T(1024)S(1)} %copy-done.2, bf16[128,3200]{1,0:T(8,128)(2,1)S(1)} %copy-done.1, f32[128]{0:T(128)S(1)} %mul.114), kind=kOutput, calls=%fused_computation.15 | convolution fusion | flops 658022400 | bytes 6566912 | tf_op jit(solution)/shard_map/dot_general | solution.py:69
  143.0 5.4 %convolution_convert_fusion.2 = bf16[128,3200]{1,0:T(8,128)(2,1)} fusion(bf16[128,800]{0,1:T(8,128)(2,1)S(1)} %fusion.8, bf16[3200,800]{1,0:T(8,128)(2,1)} %reshape.47), kind=kOutput, calls=%fused_computation.2 | convolution fusion | flops 655769600 | bytes 6144000 | tf_op jit(solution)/shard_map/dot_general | solution.py:87
  148.4 0.0 all-reduce.8.cloned.1.call-update
  148.4 0.2 all-gather.6.cloned.1.call-start
  148.7 1.3 convert_element_type.58
  150.0 0.1 dynamic_slice.10
  150.0 20.4 %reduce-scatter.8.cloned.1.call-done = bf16[400,128]{1,0:T(8,128)(2,1)} async-done(((bf16[3200,128]{1,0:T(8,128)(2,1)}), bf16[400,128]{1,0:T(8,128)(2,1)}) %reduce-scatter.8.cloned.1.call-update) | async-done | bytes 102416
  170.4 1.0 copy.36
  171.4 1.1 fusion.16
  172.5 0.1 reshape.34
  172.6 0.7 copy.27
  173.3 0.0 all-gather.6.cloned.1.call-update
  173.3 4.3 %convolution_convert_fusion.1 = bf16[3200,800]{1,0:T(8,128)(2,1)} fusion(bf16[128,800]{0,1:T(8,128)(2,1)S(1)} %fusion.8, f32[3200]{0:T(1024)S(1)} %copy-done.3, f32[128]{0:T(128)S(1)} %add_sqrt_fusion, bf16[128,3200]{1,0:T(8,128)(2,1)S(1)} %copy-done), kind=kOutput, calls=%fused_computation.1 | convolution fusion | flops 659558400 | bytes 6157312 | tf_op jit(solution)/shard_map/dot_general | solution.py:73
  177.5 4.3 %convolution_convert_fusion = bf16[800,3200]{0,1:T(8,128)(2,1)} fusion(f32[3200]{0:T(1024)S(1)} %copy-done.2, bf16[128,3200]{1,0:T(8,128)(2,1)S(1)} %copy-done.1, f32[128]{0:T(128)S(1)} %mul.114, f32[128,800]{0,1:T(8,128)S(1)} %fusion.13), kind=kOutput, calls=%fused_computation | convolution fusion | flops 660070400 | bytes 6362112 | tf_op jit(solution)/shard_map/dot_general | solution.py:76
  181.8 94.3 %fusion.20 = (bf16[112,800]{1,0:T(8,128)(2,1)}, bf16[800,112]{0,1:T(8,128)(2,1)S(1)}) fusion(bf16[3200,800]{1,0:T(8,128)(2,1)} %convolution_convert_fusion.1, bf16[800,3200]{0,1:T(8,128)(2,1)} %convolution_convert_fusion), kind=kCustom, calls=%all-reduce-scatter.2 | all-reduce-scatter fusion | flops 5734401 | bytes 10599424
  276.1 0.9 slice
  277.1 2.0 collective-permute-start.2
  279.0 2.0 collective-permute-start.1
  281.0 1.9 collective-permute-start.3
  282.9 0.2 convert_multiply_fusion.1
  283.1 1.3 fusion.21
  285.1 0.9 dynamic-update-slice
  286.0 14.5 %all-reduce = s32[64]{0:T(128)S(1)} all-reduce(s32[64]{0:T(128)S(1)} %dynamic-update-slice), channel_id=1, replica_groups=mesh['dp'=32,'mp'=8] {'dp'}, use_global_device_ids=true, to_apply=%add | all-reduce | flops 64 | bytes 512
  300.4 4.8 %collective-permute-start = (bf16[112,800]{1,0:T(8,128)(2,1)}, bf16[112,800]{1,0:T(8,128)(2,1)S(1)}, u32[]{:S(2)}, u32[]{:S(2)}) collective-permute-start(bf16[112,800]{1,0:T(8,128)(2,1)} %get-tuple-element.22), channel_id=1, source_target_pairs={{0,8},{8,16},{16,24},{24,32},{32,40},{40,48},{48,56},{56,64},{64,7... | collective-permute-start | bytes 537608
  305.2 0.7 slice.1
  305.9 4.2 %collective-permute-start.6 = (bf16[800,112]{0,1:T(8,128)(2,1)S(1)}, bf16[800,112]{0,1:T(8,128)(2,1)S(1)}, u32[]{:S(2)}, u32[]{:S(2)}) collective-permute-start(bf16[800,112]{0,1:T(8,128)(2,1)S(1)} %get-tuple-element.23), channel_id=1, source_target_pairs={{0,24},{8,32},{16,40},{24,48},{32,56},{40,64},{48,72},{56,80},{64,... | collective-permute-start | bytes 537608
  310.1 2.8 collective-permute-start.5
  312.9 0.0 collective-permute-done.2
  312.9 5.3 %collective-permute-start.4 = (bf16[800,112]{0,1:T(8,128)(2,1)S(1)}, bf16[800,112]{0,1:T(8,128)(2,1)S(1)}, u32[]{:S(2)}, u32[]{:S(2)}) collective-permute-start(bf16[800,112]{0,1:T(8,128)(2,1)S(1)} %get-tuple-element.23), channel_id=1, source_target_pairs={{0,8},{8,16},{16,24},{24,32},{32,40},{40,48},{48,56},{56,64},{64,7... | collective-permute-start | bytes 537608
  318.2 0.0 collective-permute-done.1
  318.2 2.2 collective-permute-start.7
  321.1 0.0 collective-permute-done
  321.1 8.1 %concatenate = bf16[484,800]{1,0:T(8,128)(2,1)} concatenate(bf16[36,800]{1,0:T(8,128)(2,1)} %collective-permute-done.3, bf16[112,800]{1,0:T(8,128)(2,1)} %collective-permute-done.2, bf16[112,800]{1,0:T(8,128)(2,1)} %collective-permute-done.1, bf16[112,800]{1,0:T(8,128)(2,1)S(1)} %collective-permute-done, bf16[112,800]{1,0:T(8,128)(2,1)} %get-tuple-element.22), dimensions={0} | concatenate | bytes 1548800
  329.2 6.7 %concatenate.1 = bf16[800,484]{0,1:T(8,128)(2,1)} concatenate(bf16[800,36]{0,1:T(8,128)(2,1)S(1)} %collective-permute-done.7, bf16[800,112]{0,1:T(8,128)(2,1)S(1)} %collective-permute-done.6, bf16[800,112]{0,1:T(8,128)(2,1)S(1)} %collective-permute-done.5, bf16[800,112]{0,1:T(8,128)(2,1)S(1)} %collective-permute-done.4, bf16[800,112]{0,1:T(8,128)(2,1)S(1)} %get-tuple-element.23), dimensions={1} | concatenate | bytes 1548800
  335.9 1.7 dynamic-slice_convert_fusion.1
  337.6 1.7 dynamic-slice_convert_fusion
  339.3 1.6 multiply_reduce_fusion
  340.9 0.3 fusion.14
  341.2 0.8 copy.31
  342.0 6.7 %fusion.5 = bf16[8,16,4,400]{3,0,2,1:T(8,128)(2,1)S(1)} fusion(bf16[64,16,4,400]{3,1,2,0:T(8,128)(2,1)} %all-gather.6.cloned.1.call-done, s32[64]{0:T(128)S(1)} %broadcast_subtract_fusion), kind=kOutput, calls=%fused_computation.13 | convolution fusion | flops 26419712 | bytes 3686656 | tf_op jit(solution)/shard_map/bq,qtuc->btuc/dot_general | solution.py:64
  348.6 0.3 copy.29
  348.9 1.0 copy.30
  (23 shorter events, 0.1 us)
Async XLA Ops:
  7.2 61.2 %all-gather.8.cloned.1.call-start = ((), (), s32[]{:S(2)}) async-start(), calls=%async_computation.3 | async-start | bytes 6150144 | tf_op jit(solution)/shard_map/all_gather | solution.py:26
  7.9 115.8 %all-gather.10.cloned.1.call-start = ((), (), s32[]{:S(2)}) async-start(), calls=%async_computation.4 | async-start | bytes 6150144 | tf_op jit(solution)/shard_map/all_gather | solution.py:27
  8.6 161.7 %reduce-scatter.8.cloned.1.call-start = ((), (), s32[]{:S(2)}) async-start(), calls=%async_computation.5 | async-start | bytes 921600
  10.1 163.2 %copy-start.5 = (f32[128]{0:T(128)}, f32[128]{0:T(128)S(1)}, u32[]{:S(2)}) copy-start(f32[128]{0:T(128)S(1)} %add_sqrt_fusion) | copy-start | bytes 1540
  10.1 66.7 %copy-start = (bf16[128,3200]{1,0:T(8,128)(2,1)S(1)}, bf16[128,3200]{1,0:T(8,128)(2,1)}, u32[]{:S(2)}) copy-start(bf16[128,3200]{1,0:T(8,128)(2,1)} %param.7) | copy-start | bytes 2457604
  10.1 66.7 %copy-start.3 = (f32[3200]{0:T(1024)S(1)}, f32[3200]{0:T(1024)}, u32[]{:S(2)}) copy-start(f32[3200]{0:T(1024)} %param.9) | copy-start | bytes 38404
  136.6 1.4 copy-start.7
  136.6 1.6 copy-start.1
  136.6 1.6 copy-start.2
  137.9 201.3 %all-reduce.8.cloned.1.call-start = ((), (), s32[]{:S(2)}) async-start(), calls=%async_computation.2 | async-start | bytes 1638400 | tf_op jit(solution)/shard_map/psum | solution.py:90
  148.4 193.5 %all-gather.6.cloned.1.call-start = ((), (), s32[]{:S(2)}) async-start(), calls=%async_computation.1 | async-start | bytes 4325376 | tf_op jit(solution)/shard_map/all_gather | solution.py:57
  277.1 35.8 %collective-permute-start.2 = (bf16[112,800]{1,0:T(8,128)(2,1)}, bf16[112,800]{1,0:T(8,128)(2,1)}, u32[]{:S(2)}, u32[]{:S(2)}) collective-permute-start(bf16[112,800]{1,0:T(8,128)(2,1)} %get-tuple-element.22), channel_id=1, source_target_pairs={{0,24},{8,32},{16,40},{24,48},{32,56},{40,64},{48,72},{56,80},{64,... | collective-permute-start | bytes 537608
  279.0 39.1 %collective-permute-start.1 = (bf16[112,800]{1,0:T(8,128)(2,1)}, bf16[112,800]{1,0:T(8,128)(2,1)}, u32[]{:S(2)}, u32[]{:S(2)}) collective-permute-start(bf16[112,800]{1,0:T(8,128)(2,1)} %get-tuple-element.22), channel_id=1, source_target_pairs={{0,16},{8,24},{16,32},{24,40},{32,48},{40,56},{48,64},{56,72},{64,... | collective-permute-start | bytes 537608
  281.0 29.1 %collective-permute-start.3 = (bf16[36,800]{1,0:T(8,128)(2,1)S(1)}, bf16[36,800]{1,0:T(8,128)(2,1)}, u32[]{:S(2)}, u32[]{:S(2)}) collective-permute-start(bf16[36,800]{1,0:T(8,128)(2,1)S(1)} %slice), channel_id=1, source_target_pairs={{0,32},{8,40},{16,48},{24,56},{32,64},{40,72},{48,80},{56,88},{64,... | collective-permute-start | bytes 172808
  300.4 20.7 %collective-permute-start = (bf16[112,800]{1,0:T(8,128)(2,1)}, bf16[112,800]{1,0:T(8,128)(2,1)S(1)}, u32[]{:S(2)}, u32[]{:S(2)}) collective-permute-start(bf16[112,800]{1,0:T(8,128)(2,1)} %get-tuple-element.22), channel_id=1, source_target_pairs={{0,8},{8,16},{16,24},{24,32},{32,40},{40,48},{48,56},{56,64},{64,7... | collective-permute-start | bytes 537608
  305.9 23.3 %collective-permute-start.6 = (bf16[800,112]{0,1:T(8,128)(2,1)S(1)}, bf16[800,112]{0,1:T(8,128)(2,1)S(1)}, u32[]{:S(2)}, u32[]{:S(2)}) collective-permute-start(bf16[800,112]{0,1:T(8,128)(2,1)S(1)} %get-tuple-element.23), channel_id=1, source_target_pairs={{0,24},{8,32},{16,40},{24,48},{32,56},{40,64},{48,72},{56,80},{64,... | collective-permute-start | bytes 537608
  310.1 19.1 %collective-permute-start.5 = (bf16[800,112]{0,1:T(8,128)(2,1)S(1)}, bf16[800,112]{0,1:T(8,128)(2,1)S(1)}, u32[]{:S(2)}, u32[]{:S(2)}) collective-permute-start(bf16[800,112]{0,1:T(8,128)(2,1)S(1)} %get-tuple-element.23), channel_id=1, source_target_pairs={{0,16},{8,24},{16,32},{24,40},{32,48},{40,56},{48,64},{56,72},{64,... | collective-permute-start | bytes 537608
  312.9 16.3 %collective-permute-start.4 = (bf16[800,112]{0,1:T(8,128)(2,1)S(1)}, bf16[800,112]{0,1:T(8,128)(2,1)S(1)}, u32[]{:S(2)}, u32[]{:S(2)}) collective-permute-start(bf16[800,112]{0,1:T(8,128)(2,1)S(1)} %get-tuple-element.23), channel_id=1, source_target_pairs={{0,8},{8,16},{16,24},{24,32},{32,40},{40,48},{48,56},{56,64},{64,7... | collective-permute-start | bytes 537608
  318.2 11.0 %collective-permute-start.7 = (bf16[800,36]{0,1:T(8,128)(2,1)}, bf16[800,36]{0,1:T(8,128)(2,1)S(1)}, u32[]{:S(2)}, u32[]{:S(2)}) collective-permute-start(bf16[800,36]{0,1:T(8,128)(2,1)} %slice.1), channel_id=1, source_target_pairs={{0,32},{8,40},{16,48},{24,56},{32,64},{40,72},{48,80},{56,88},{64,... | collective-permute-start | bytes 172808
  329.2 10.1 %copy-start.4 = (f32[3200]{0:T(1024)S(1)}, f32[3200]{0:T(1024)}, u32[]{:S(2)}) copy-start(f32[3200]{0:T(1024)} %param.9) | copy-start | bytes 38404
  329.2 10.1 %copy-start.6 = (f32[128]{0:T(128)S(1)}, f32[128]{0:T(128)}, u32[]{:S(2)}) copy-start(f32[128]{0:T(128)} %copy-done.5) | copy-start | bytes 1540
Sparse Core Ops, SparseCore 0:
  10.5 57.8 all-gather.7
  70.9 52.7 all-gather.9
  138.1 32.2 reduce-scatter.7
  172.7 73.7 all-reduce.7
  249.5 58.8 all-gather.5
where the time goes:
time: 358 us; the launch traced here: 356 us
  waiting for transfers between devices  122 us (34%)
  blocking collectives  109 us (30%)
  local copies, waits for them, and re-layouts  40.6 us (11%)
  matrix products  34.8 us (10%)
  starting transfers between devices  25.5 us (7%)
  between operations  15.3 us (4%)
  other arithmetic  9.33 us (3%)
    unnamed x2, blocking collectives  109 us
    all_gather x1, waiting for transfers between devices, shards(): lax.all_gather(w_in, 'dp', axis=0, tiled=True)  58.3 us
    all_gather x1, waiting for transfers between devices, shards(): lax.all_gather(w_out, 'dp', axis=1, tiled=True)  42 us
    unnamed x29, local copies, waits for them, and re-layouts  39.3 us
    unnamed x9, starting transfers between devices  25.2 us
    unnamed x14, waiting for transfers between devices  21.8 us
  transfers between devices with their start and end apart: 13, of which 3 were waited for; matrix products, arithmetic and copies ran while one was open for 44% of the time, Pallas kernels for 0%

commit v1 on v0

v1 whole, which is shorter than its diff:
```python
import functools
import jax
import jax.numpy as jnp
from jax import lax
from jax.experimental import pallas as pl
from jax.experimental.pallas import tpu as pltpu
from jax.sharding import PartitionSpec as P

BLK = 8
FE = 100
HH = 400
UR = 208
PK = 656
HA = 336
MESH = pl.DeviceIdType.MESH
F32 = jnp.float32
BF = jnp.bfloat16


def fold_tail(tail):
    tail = jnp.concatenate([tail, jnp.zeros((16, 128), F32)], axis=0)
    out = tail[0:32]
    for g in range(1, 7):
        out = out + pltpu.roll(tail[32 * g : 32 * g + 32], 16 * g, 1)
    return out


def unfold_tail(packed):
    packed = packed.astype(F32)
    rows = [packed] + [pltpu.roll(packed, 128 - 16 * g, 1) for g in range(1, 7)]
    return jnp.concatenate(rows, axis=0)[:UR]


def kernel(
    wu, acts, base, scale, g_out, z_out, v_out,
    U, C2, CT, hacc, S, ST, PG, rb1, rb2, ra1, ra2, fin, M, MR, zrm, zrp, V, cen,
    ag_s, ag_r, rs_s, rs_r, vg_s, vg_r, vf_s, vf_r, sq_s, sq_r, zz_s, zz_r, mi_s, mi_r, loc,
):
    dp = lax.axis_index("dp")
    z = lax.axis_index("mp")
    c = lax.rem(dp, 2)
    x = lax.rem(dp // 2, 4)
    y = dp // 8
    me = y * 4 + x

    def chip_of(u, da, db):
        if u == 0:
            return lax.rem(y + db, 4) * 4 + lax.rem(x + da, 4)
        return lax.rem(y + da, 4) * 4 + lax.rem(x + db, 4)

    def dev(u, da, db):
        return (chip_of(u, da, db) * 2 + c, z)

    def zdev(dz):
        return (dp, lax.rem(z + dz, 8))

    sib = (me * 2 + 1 - c, z)
    nbrs = [sib, dev(0, 1, 0), dev(0, 3, 0), dev(0, 0, 1), dev(0, 0, 3), zdev(1), zdev(7)]

    def rc(src, dst, ss, rs, d):
        return pltpu.make_async_remote_copy(
            src_ref=src, dst_ref=dst, send_sem=ss, recv_sem=rs, device_id=d, device_id_type=MESH
        )

    def core_of(u):
        return c if u == 0 else 1 - c

    def uidx(u, da, db):
        return chip_of(u, da, db) * 2 + core_of(u)

    def da_of(k):
        return k + k // 2 - 2 * (k // 3)

    barrier = pltpu.get_barrier_semaphore()
    for d in nbrs:
        pl.semaphore_signal(barrier, inc=1, device_id=d, device_id_type=MESH)
    pl.semaphore_wait(barrier, len(nbrs))

    class Gather:
        def __init__(self, slot, split, ss, rs):
            self.slot, self.split, self.ss, self.rs = slot, split, ss, rs

        def copy(self, u, m, da, db, d, part=None):
            ref = self.slot(u, da, db, part)
            return rc(ref, ref, self.ss.at[u, m], self.rs.at[u, m], d)

        def start(self, u):
            for m, d in ((0, dev(u, 1, 0)), (1, dev(u, 3, 0)), (4, dev(u, 0, 1)), (8, dev(u, 0, 3))):
                self.copy(u, m, 0, 0, d).start()

        def wait(self, u, m, da, db, part=None):
            self.copy(u, m, da, db, sib, part).wait_recv()

        def near(self, u):
            self.wait(u, 0, 3, 0)
            self.copy(u, 2, 3, 0, dev(u, 1, 0), 0).start()
            self.copy(u, 6, 3, 0, dev(u, 0, 1)).start()
            self.copy(u, 10, 3, 0, dev(u, 0, 3)).start()
            self.wait(u, 1, 1, 0)
            self.copy(u, 3, 1, 0, dev(u, 3, 0), 1).start()
            self.copy(u, 5, 1, 0, dev(u, 0, 1)).start()
            self.copy(u, 9, 1, 0, dev(u, 0, 3)).start()

        def far(self, u):
            self.wait(u, 2, 2, 0, 0)
            self.wait(u, 3, 2, 0, 1)
            self.copy(u, 7, 2, 0, dev(u, 0, 1)).start()
            self.copy(u, 11, 2, 0, dev(u, 0, 3)).start()

        def side(self, u, k):
            da = da_of(k)
            self.wait(u, 4 + k, da, 3)
            self.wait(u, 8 + k, da, 1)

            @pl.when(k < 2)
            def _():
                self.copy(u, 12 + k, da, 3, dev(u, 0, 1)).start()

            @pl.when(k >= 2)
            def _():
                self.copy(u, 12 + k, da, 1, dev(u, 0, 3)).start()

        def last(self, u, k):
            self.wait(u, 12 + k, da_of(k), 2)

        def done(self):
            for u in (0, 1):
                for m in (2,):
                    self.copy(u, m, 0, 0, sib, 0).wait_send()
                for m in (3,):
                    self.copy(u, m, 0, 0, sib, 1).wait_send()
                for m in (0, 1) + tuple(range(4, 16)):
                    self.copy(u, m, 0, 0, sib).wait_send()

    def wslot(u, da, db, part):
        ref = U.at[uidx(u, da, db)]
        if part is None:
            return ref
        return ref.at[pl.ds(0, HA)] if part == 0 else ref.at[pl.ds(HA, PK - HA)]

    ag = Gather(wslot, HA, ag_s, ag_r)

    own = pltpu.make_async_copy(wu.at[c], U.at[me * 2 + c], loc.at[0])
    own.start()
    to_sib = rc(wu.at[1 - c], U.at[me * 2 + c], mi_s.at[0], mi_r.at[0], sib)
    to_sib.start()
    act_own = pltpu.make_async_copy(acts, C2.at[c], loc.at[1])
    act_own.start()
    act_sib = rc(acts, C2.at[c], mi_s.at[1], mi_r.at[1], sib)
    own.wait()
    ag.start(0)
    rc(wu.at[0], U.at[me * 2 + 1 - c], mi_s.at[0], mi_r.at[0], sib).wait_recv()
    ag.start(1)
    act_sib.start()
    hacc[...] = jnp.zeros_like(hacc)
    act_own.wait()
    rc(acts, C2.at[1 - c], mi_s.at[1], mi_r.at[1], sib).wait_recv()

    def weight(i):
        w = U[i]
        tail = unfold_tail(w[624:656]).astype(BF)
        return jnp.concatenate([w[0:208], w[208:416], w[416:624], tail], axis=1)

    def up(i):
        act = jnp.concatenate([C2[0, i], C2[1, i]], axis=0)
        CT[i] = act.T[:UR]
        a = act[:, :UR]
        first = lax.broadcasted_iota(jnp.int32, a.shape, 1) < FE
        zero = jnp.zeros_like(a)
        lhs = jnp.concatenate([jnp.where(first, a, zero), jnp.where(first, zero, a)], axis=0)
        hacc[...] += jnp.dot(lhs, weight(i), preferred_element_type=F32)

    for u in (0, 1):
        up(uidx(u, 0, 0))
    for u in (0, 1):
        ag.near(u)
    for u in (0, 1):
        up(uidx(u, 3, 0))
        up(uidx(u, 1, 0))
    for u in (0, 1):
        ag.far(u)
    for u in (0, 1):
        up(uidx(u, 2, 0))

    def side_step(k, carry):
        for u in (0, 1):
            ag.side(u, k)
        for u in (0, 1):
            up(uidx(u, da_of(k), 3))
            up(uidx(u, da_of(k), 1))
        return carry

    lax.fori_loop(0, 4, side_step, 0)

    def last_step(k, carry):
        for u in (0, 1):
            ag.last(u, k)
            up(uidx(u, da_of(k), 2))
        return carry

    lax.fori_loop(0, 4, last_step, 0)

    def gelu_step(r, carry):
        r0 = pl.multiple_of(r * 32, 32)
        h = hacc[pl.ds(r0, 32), :]
        gh = hacc[pl.ds(r0 + 256, 32), :]
        live = lax.broadcasted_iota(jnp.int32, h.shape, 1) < HH
        cumul = 0.5 * (1.0 + lax.erf(h * 0.7071067811865476))
        density = jnp.exp(-0.5 * h * h) * 0.3989422804014327
        ho = jnp.where(live, h * cumul, 0.0).astype(BF)
        gi = jnp.where(live, gh * (cumul + h * density), 0.0).astype(BF)
        S[pl.ds(r0, 32), :] = gi
        S[pl.ds(r0 + 256, 32), :] = ho
        row = jnp.sum(gi.astype(F32) * jnp.where(live, h, 0.0), axis=1, keepdims=True)
        cen[pl.ds(r0, 32), :] = jnp.broadcast_to(row, (32, 128))
        return carry

    lax.fori_loop(0, 8, gelu_step, 0)
    ST[...] = S[...].T
    center = cen[...].T[0:1]
    cen_hi = center.astype(BF).astype(F32)
    cen_lo = center - cen_hi

    def down(i):
        ct = CT[i]
        first = lax.broadcasted_iota(jnp.int32, ct.shape, 0) < FE
        zero = jnp.zeros_like(ct)
        lhs = jnp.concatenate([jnp.where(first, ct, zero), jnp.where(first, zero, ct)], axis=1)
        out = jnp.dot(lhs, S[...], preferred_element_type=F32)
        return [out[:, 0:128], out[:, 128:256], out[:, 256:384], fold_tail(out[:, 384:512])]

    ROWS4 = ((0, 208), (208, 416), (416, 624), (624, 656))

    def store_unit(i, *adds):
        for (lo, hi), part in zip(ROWS4, down(i)):
            for ref in adds:
                part = part + ref[lo:hi].astype(F32)
            PG[i, lo:hi] = part.astype(BF)

    def rs(u, m, i, dst, d, lo=0, hi=PK):
        return rc(PG.at[i, pl.ds(lo, hi - lo)], dst, rs_s.at[u, m], rs_r.at[u, m], d)

    def first_down(k, carry):
        for u in (0, 1):
            i = uidx(u, da_of(k), 2)
            store_unit(i)

            @pl.when(k < 2)
            def _():
                rs(u, k, i, rb1.at[u, k], dev(u, 0, 1)).start()

            @pl.when(k >= 2)
            def _():
                rs(u, k, i, rb1.at[u, k], dev(u, 0, 3)).start()

        return carry

    lax.fori_loop(0, 4, first_down, 0)

    def zblk(r):
        return lax.rem(z + r, 8)

    def mix(b):
        def body(j, carry):
            i = b * 4 + j
            out = jnp.dot(weight(i), ST[...], preferred_element_type=F32)
            row = lax.broadcasted_iota(jnp.int32, (UR, 256), 0)
            m = jnp.where(row < FE, out[:, :256], out[:, 256:])
            m = jnp.where(row == 200, cen_hi, jnp.where(row == 201, cen_lo, m)).astype(BF)
            M[0, i] = m[:, :128]
            M[1, i] = m[:, 128:]
            return carry

        lax.fori_loop(0, 4, body, 0)

    def zr_of(s):
        return 4 + (1 - 2 * (s % 2)) * ((s + 1) // 2) - 8 * (s // 8)

    def zsend_copy(s, r):
        b = zblk(r)
        return rc(M.at[1 - c, pl.ds(4 * b, 4)], MR.at[pl.ds(4 * b, 4)], sq_s.at[s], sq_r.at[s], sib)

    zorder = (4, 3, 5, 2, 6, 1, 7, 0)

    def mix_step(s, carry):
        h = (s + 1) // 2
        r = 4 + h - 2 * h * (s % 2)
        mix(zblk(r))
        zsend_copy(s, r).start()
        return carry

    lax.fori_loop(0, 8, mix_step, 0)

    def combine(r, *adds):
        b = zblk(r)

        def body(j, carry):
            i = b * 4 + j
            t = M[c, i].astype(F32) + MR[i].astype(F32)
            for ref in adds:
                t = t + ref[j].astype(F32)
            M[c, i] = t.astype(BF)
            return carry

        lax.fori_loop(0, 4, body, 0)

    def zcopy_m(j):
        return rc(M.at[c, pl.ds(4 * zblk(4 + j), 4)], zrm.at[j], zz_s.at[j], zz_r.at[j], zdev(7))

    def zcopy_p(j):
        return rc(M.at[c, pl.ds(4 * zblk(3 - j), 4)], zrp.at[j], zz_s.at[4 + j], zz_r.at[4 + j], zdev(1))

    def zstep(j):
        s = 2 * j
        zsend_copy(s, 4 + j).wait_recv()
        if j == 0:
            combine(4 + j)
        else:
            zcopy_m(j - 1).wait_recv()
            combine(4 + j, zrm.at[j - 1])
        zcopy_m(j).start()
        if j < 3:
            zsend_copy(s + 1, 3 - j).wait_recv()
            if j == 0:
                combine(3 - j)
            else:
                zcopy_p(j - 1).wait_recv()
                combine(3 - j, zrp.at[j - 1])
            zcopy_p(j).start()

    zstep(0)

    def second_down(k, carry):
        for u in (0, 1):
            ip = uidx(u, da_of(k), 1)
            im = uidx(u, da_of(k), 3)

            rs(u, k, ip, rb1.at[u, k], sib).wait_recv()

            @pl.when(k < 2)
            def _():
                store_unit(ip, rb1.at[u, k])
                store_unit(im)

            @pl.when(k >= 2)
            def _():
                store_unit(ip)
                store_unit(im, rb1.at[u, k])

            rs(u, 4 + k, ip, rb2.at[u, 0, k], dev(u, 0, 1)).start()
            rs(u, 8 + k, im, rb2.at[u, 1, k], dev(u, 0, 3)).start()
        return carry

    lax.fori_loop(0, 2, second_down, 0)
    zstep(1)
    lax.fori_loop(2, 4, second_down, 0)
    zstep(2)

    def third_wait(u, k):
        rs(u, 4 + k, uidx(u, 0, 0), rb2.at[u, 0, k], sib).wait_recv()
        rs(u, 8 + k, uidx(u, 0, 0), rb2.at[u, 1, k], sib).wait_recv()

    def third(u, k):
        third_wait(u, k)
        i = uidx(u, da_of(k), 0)
        store_unit(i, rb2.at[u, 0, k], rb2.at[u, 1, k])
        return i

    for u in (0, 1):
        i = third(u, 3)
        rs(u, 12, i, ra1.at[u, pl.ds(0, HA)], dev(u, 1, 0), 0, HA).start()
        rs(u, 13, i, ra1.at[u, pl.ds(HA, PK - HA)], dev(u, 3, 0), HA, PK).start()
    zstep(3)
    for u in (0, 1):
        third(u, 1)
        third(u, 2)
    for u in (0, 1):
        i = uidx(u, 1, 0)
        rs(u, 12, i, ra1.at[u, pl.ds(0, HA)], sib, 0, HA).wait_recv()
        PG[i, 0:HA] = (PG[i, 0:HA].astype(F32) + ra1[u, 0:HA].astype(F32)).astype(BF)
        rs(u, 14, i, ra2.at[u, 0], dev(u, 1, 0)).start()
        i = uidx(u, 3, 0)
        rs(u, 13, i, ra1.at[u, pl.ds(HA, PK - HA)], sib, HA, PK).wait_recv()
        PG[i, HA:PK] = (PG[i, HA:PK].astype(F32) + ra1[u, HA:PK].astype(F32)).astype(BF)
        rs(u, 15, i, ra2.at[u, 1], dev(u, 3, 0)).start()

    zcopy_m(3).wait_recv()
    zcopy_p(2).wait_recv()
    zsend_copy(7, 0).wait_recv()
    for j in range(4):
        i = z * 4 + j
        t = M[c, i].astype(F32) + MR[i].astype(F32) + zrm[3, j].astype(F32) + zrp[2, j].astype(F32)
        z_out[j] = t
        V[c, me, pl.ds(112 * j, 112), :] = (base[j] + scale[j] * t[96:208]).astype(BF)

    def vslot(u, da, db, part):
        lo = 224 * u
        n = 224
        if part is not None:
            lo, n = lo + 112 * part, 112
        return V.at[c, chip_of(u, da, db), pl.ds(lo, n)]

    vg = Gather(vslot, 112, vg_s, vg_r)

    def fwd(u, da, db):
        ch = chip_of(u, da, db)
        ref = V.at[c, ch, pl.ds(224 * u, 224)]
        return rc(ref, ref, vf_s.at[u, ch], vf_r.at[u, ch], sib)

    for u in (0, 1):
        vg.start(u)
    for u in (0, 1):
        fwd(u, 0, 0).start()

    def finish(u):
        third_wait(u, 0)
        i = uidx(u, 0, 0)
        parts = down(i)
        rs(u, 14, i, ra2.at[u, 0], sib).wait_recv()
        rs(u, 15, i, ra2.at[u, 1], sib).wait_recv()
        out = []
        for (lo, hi), part in zip(ROWS4, parts):
            for ref in (rb2.at[u, 0, 0], rb2.at[u, 1, 0], ra2.at[u, 0], ra2.at[u, 1]):
                part = part + ref[lo:hi].astype(F32)
            out.append(part)
        return i, out

    i, parts = finish(1)
    for (lo, hi), part in zip(ROWS4, parts):
        PG[i, lo:hi] = part.astype(BF)
    to_fin = rc(PG.at[i], fin, mi_s.at[2], mi_r.at[2], sib)
    to_fin.start()
    _, parts = finish(0)
    for t in range(3):
        g_out[c, :, 128 * t : 128 * t + 128] = parts[t]
    g_out[c, :, 384:512] = unfold_tail(parts[3])

    for u in (0, 1):
        vg.near(u)
    for u in (0, 1):
        fwd(u, 3, 0).start()
        fwd(u, 1, 0).start()
    for u in (0, 1):
        vg.far(u)
        fwd(u, 2, 0).start()

    def vside(k, carry):
        for u in (0, 1):
            vg.side(u, k)
            fwd(u, da_of(k), 3).start()
            fwd(u, da_of(k), 1).start()
        return carry

    lax.fori_loop(0, 4, vside, 0)

    to_fin.wait_recv()
    for t in range(3):
        g_out[1 - c, :, 128 * t : 128 * t + 128] = fin[208 * t : 208 * t + 208].astype(F32)
    g_out[1 - c, :, 384:512] = unfold_tail(fin[624:656])

    def vlast(k, carry):
        for u in (0, 1):
            vg.last(u, k)
            fwd(u, da_of(k), 2).start()
        return carry

    lax.fori_loop(0, 4, vlast, 0)

    def vfwd_wait(ch, carry):
        for u in (0, 1):
            ref = V.at[1 - c, ch, pl.ds(224 * u, 224)]
            d = rc(ref, ref, vf_s.at[u, ch], vf_r.at[u, ch], sib)
            d.wait_recv()
            d.wait_send()
        return carry

    lax.fori_loop(0, 16, vfwd_wait, 0)
    vcopy = pltpu.make_async_copy(V, v_out, loc.at[2])
    vcopy.start()

    ag.done()
    vg.done()
    to_sib.wait_send()
    act_sib.wait_send()
    to_fin.wait_send()
    for s in range(8):
        zsend_copy(s, zorder[s]).wait_send()
    for j in range(4):
        zcopy_m(j).wait_send()
    for j in range(3):
        zcopy_p(j).wait_send()
    for u in (0, 1):
        i = uidx(u, 0, 0)
        for m in range(16):
            lo, hi = (0, HA) if m == 12 else (HA, PK) if m == 13 else (0, PK)
            dst = ra1.at[u, pl.ds(lo, hi - lo)]
            rs(u, m, i, dst, sib, lo, hi).wait_send()
    vcopy.wait()


def mega(wu, acts, base, scale):
    dma = pltpu.SemaphoreType.DMA
    vm = pl.BlockSpec(memory_space=pltpu.VMEM)
    return pl.pallas_call(
        kernel,
        out_shape=(
            jax.ShapeDtypeStruct((2, UR, 512), F32),
            jax.ShapeDtypeStruct((4, UR, 128), F32),
            jax.ShapeDtypeStruct((2, 16, 448, 128), BF),
        ),
        in_specs=[vm] * 4,
        out_specs=(vm, vm, pl.BlockSpec(memory_space=pl.ANY)),
        scratch_shapes=[
            pltpu.VMEM((32, PK, 128), BF),
            pltpu.VMEM((2, 32, 128, 256), BF),
            pltpu.VMEM((32, UR, 256), BF),
            pltpu.VMEM((512, 512), F32),
            pltpu.VMEM((512, 512), BF),
            pltpu.VMEM((512, 512), BF),
            pltpu.VMEM((32, PK, 128), BF),
            pltpu.VMEM((2, 4, PK, 128), BF),
            pltpu.VMEM((2, 2, 4, PK, 128), BF),
            pltpu.VMEM((2, PK, 128), BF),
            pltpu.VMEM((2, 2, PK, 128), BF),
            pltpu.VMEM((PK, 128), BF),
            pltpu.VMEM((2, 32, UR, 128), BF),
            pltpu.VMEM((32, UR, 128), BF),
            pltpu.VMEM((4, 4, UR, 128), BF),
            pltpu.VMEM((3, 4, UR, 128), BF),
            pltpu.VMEM((2, 16, 448, 128), BF),
            pltpu.VMEM((256, 128), F32),
            dma((2, 16)), dma((2, 16)),
            dma((2, 16)), dma((2, 16)),
            dma((2, 16)), dma((2, 16)),
            dma((2, 16)), dma((2, 16)),
            dma((8,)), dma((8,)),
            dma((7,)), dma((7,)),
            dma((3,)), dma((3,)),
            dma((3,)),
        ],
        compiler_params=pltpu.CompilerParams(
            collective_id=0, has_side_effects=True, vmem_limit_bytes=60 * 2**20
        ),
    )(wu, acts, base, scale)


def columns(array, count, axis):
    return lax.dynamic_slice_in_dim(array, lax.axis_index("mp") * count, count, axis)


def pack_units(w_in, w_out):
    both = jnp.concatenate([w_in, w_out.T, jnp.zeros((8, 2 * HH), BF)], axis=0)
    halves = []
    for h in (0, 1):
        part = both[:, HH * h : HH * h + HH]
        tail = jnp.pad(part[:, 384:], ((0, 48), (0, 0)))
        tail = tail.reshape(8, 32, 16).transpose(1, 0, 2).reshape(32, 128)
        halves.append(
            jnp.concatenate([part[:, 0:128], part[:, 128:256], part[:, 256:384], tail], axis=0)
        )
    return jnp.stack(halves)


def shards(patches, upstream, norm_gain, layer_scale, w_in, w_out, slot_block):
    rows, width = patches.shape
    share = width // lax.axis_size("mp")
    wu = pack_units(w_in, w_out)
    inputs = patches.astype(F32)
    root_mean = jnp.sqrt(jnp.mean(inputs * inputs, axis=-1, keepdims=True) + 1e-06)
    normed = (inputs / root_mean * norm_gain).astype(BF)
    live_row = jnp.repeat((slot_block >= 0).astype(F32), rows // 2)[:, None]
    grad_mixed = (upstream.astype(F32) * live_row * layer_scale).astype(BF)
    acts = jnp.concatenate(
        [
            normed.reshape(rows, 32, FE),
            grad_mixed.reshape(rows, 32, FE),
            jnp.zeros((rows, 32, 256 - 2 * FE), BF),
        ],
        axis=2,
    ).transpose(1, 0, 2)
    mine = columns(patches, share, 1).astype(F32)
    blocks_row = jnp.repeat(slot_block, rows // 2).astype(F32)[None, None, :]
    base = jnp.concatenate(
        [
            jnp.zeros((4, 4, rows), F32),
            mine.T.reshape(4, FE, rows),
            jnp.broadcast_to(blocks_row, (4, 1, rows)),
            jnp.zeros((4, 7, rows), F32),
        ],
        axis=1,
    )
    scale = jnp.pad(columns(layer_scale, share, 0).reshape(4, FE), ((0, 0), (4, 8)))
    scale = jnp.broadcast_to(scale[:, :, None], (4, 112, rows))
    g, zsum, arrived = mega(wu, acts, base, scale)

    grad_w_in = jnp.concatenate([g[0, :FE, :HH], g[1, :FE, :HH]], axis=1)
    grad_w_out = jnp.concatenate([g[0, FE : 2 * FE, :HH], g[1, FE : 2 * FE, :HH]], axis=1).T

    tiles = arrived.reshape(32, 4, 112, 2, 64)
    blocks = tiles[:, 0, 104, :, 0].astype(jnp.int32)
    blocks = blocks.reshape(64)
    want = lax.axis_index("dp") * BLK + jnp.arange(BLK, dtype=jnp.int32)
    hit = blocks[None, :] == want[:, None]
    found = jnp.any(hit, axis=1)
    which = jnp.argmax(hit, axis=1)
    flat = tiles[:, :, 4:104].transpose(0, 3, 1, 2, 4).reshape(64, share, 64)
    tok = jnp.where(found[:, None, None], jnp.take(flat, which, axis=0), 0)
    tok = tok.transpose(0, 2, 1)
    vision = (
        tok.reshape(BLK, 2, 16, 2, share).transpose(0, 2, 1, 3, 4).reshape(BLK * 16, 4, share)
    )

    grad_normed = zsum[:, :FE].reshape(share, rows).T
    center = ((zsum[0, 200] + zsum[0, 201]) / width)[:, None]
    unit_mine = mine / root_mean
    live_mine = columns(upstream, share, 1).astype(F32) * live_row
    scaled = columns(norm_gain, share, 0) * grad_normed
    grad_patches = (live_mine + (scaled - unit_mine * center) / root_mean).astype(BF)
    return (vision, grad_patches, grad_w_in, grad_w_out)


def solution(mesh):
    return jax.shard_map(
        shards,
        mesh=mesh,
        in_specs=(P("dp", None), P("dp", None), P(), P(), P("dp", "mp"), P("mp", "dp"), P("dp")),
        out_specs=(P("dp", None, "mp"), P("dp", "mp"), P("dp", "mp"), P("mp", "dp")),
        check_vma=False,
    )
```

time: 358 us -> 167 us (0.47)
  waiting for transfers between devices: 122 us -> 0 us
  blocking collectives: 109 us -> 0 us
  Pallas kernels: 0 us -> 103 us
  matrix products: 34.8 us -> 0 us
  starting transfers between devices: 25.5 us -> 0 us
  between operations: 15.3 us -> 0.9 us
  local copies, waits for them, and re-layouts: 40.6 us -> 48 us
  other arithmetic: 9.33 us -> 13.8 us
    unnamed x2 -> x0, blocking collectives: 109 us -> none
    pallas_call x0 -> x1, Pallas kernels: none -> 103 us  [mega(): pl.pallas_call(kernel, out_shape=(jax.ShapeDtypeStruct((2, UR, 512), F32)...]
    all_gather x3 -> x0, waiting for transfers between devices: 100 us -> none  [the longest x1 58.3 us: shards(): lax.all_gather(w_in, 'dp', axis=0, tiled=True)]
    unnamed x29 -> x17, local copies, waits for them, and re-layouts: 39.3 us -> 1.95 us
    dot_general x7 -> x0, matrix products: 34.8 us -> none  [the longest x1 6.66 us: shards(): jnp.einsum('bq,qtuc->btuc', placing, arrived, preferred_element_type=jnp....]
    unnamed x9 -> x0, starting transfers between devices: 25.2 us -> none
    reshape x1 -> x13, local copies, waits for them, and re-layouts: 0.07 us -> 24.6 us  [the longest x1 7.82 us: shards(): flat = tiles[:, :, 4:104].transpose(0, 3, 1, 2, 4).reshape(64, share, 64)]
    unnamed x14 -> x0, waiting for transfers between devices: 21.8 us -> none
  transfers between devices with their start and end apart: 13 -> 0, of which waited for: 3 -> 0; matrix products, arithmetic and copies ran while one was open for 44% -> 0% of each run, Pallas kernels for 0% -> 0%
where the time goes in v1:
time: 167 us; the launch traced here: 166 us
  Pallas kernels  103 us (62%)
  local copies, waits for them, and re-layouts  48 us (29%)
  other arithmetic  13.8 us (8%)
    pallas_call x1, Pallas kernels, mega(): pl.pallas_call(kernel, out_shape=(jax.ShapeDtypeStruct((2, UR, 512), F32)...  103 us
    reshape x1, local copies, waits for them, and re-layouts, shards(): flat = tiles[:, :, 4:104].transpose(0, 3, 1, 2, 4).reshape(64, share, 64)  7.82 us
    reshape x1, local copies, waits for them, and re-layouts, shards(): tiles = arrived.reshape(32, 4, 112, 2, 64)  7.64 us
    transpose x1, local copies, waits for them, and re-layouts, shards(): flat = tiles[:, :, 4:104].transpose(0, 3, 1, 2, 4).reshape(64, share, 64)  6.4 us
    pallas_call x1, local copies, waits for them, and re-layouts, mega(): pl.pallas_call(kernel, out_shape=(jax.ShapeDtypeStruct((2, UR, 512), F32)...  6.1 us
    reshape x2, local copies, waits for them, and re-layouts, shards(): normed.reshape(rows, 32, FE)  4.35 us
    reshape x2, local copies, waits for them, and re-layouts, shards(): grad_mixed.reshape(rows, 32, FE)  4.35 us

profile of v1, /device:TPU:1, one launch (start us, length us, event | category | flops | bytes accessed | tf_op | source)
XLA Modules:
  0.0 166.1 jit_solution(17830980683280317888)
XLA Ops:
  0.6 0.0 copy-start.3
  0.6 0.0 copy-start.4
  0.7 0.7 convert_element_type.58
  1.4 0.1 broadcast_in_dim.65
  1.5 0.1 convert_element_type.59
  1.5 0.7 compare_convert_fusion
  2.2 0.1 broadcast_in_dim.62
  2.3 0.1 mul.68
  2.4 1.4 fusion
  3.8 0.1 pad.24.clone
  3.8 0.1 pad.37.clone
  3.9 0.1 pad.21.clone
  4.0 0.8 dynamic_slice.15
  4.8 0.8 dynamic_slice.13
  5.6 0.1 reshape.106
  5.6 0.1 pad.13
  5.7 0.8 broadcast_in_dim.68.scale
  6.5 1.1 constant_dynamic-slice_fusion
  7.7 0.1 copy.49
  7.8 0.1 copy.48
  8.0 0.0 copy-start
  8.0 0.0 copy-start.5
  8.0 0.8 maximum_maximum_fusion.1.base
  8.8 0.0 copy-done.4
  8.8 0.1 maximum_maximum_fusion
  8.9 0.1 fusion.10
  9.0 0.1 fusion.9
  9.2 0.1 copy.30
  9.3 0.1 copy.31
  9.4 0.1 copy.32
  9.5 0.1 copy.33
  9.6 0.1 maximum_bitcast_fusion.2
  9.6 0.8 pad_maximum_fusion.1.wu
  10.4 0.3 fusion.2
  10.6 0.0 copy-start.6
  10.7 3.9 %reshape.122 = bf16[128,32,100]{2,1,0:T(8,128)(2,1)S(1)} reshape(bf16[128,3200]{1,0:T(8,128)(2,1)S(1)} %fusion.2) | data formatting | bytes 1638400 | tf_op jit(solution)/shard_map/reshape | solution.py:575
  14.6 0.0 copy-start.1
  14.6 0.4 copy.36
  15.0 0.7 copy-done.1
  15.8 0.3 multiply_convert_fusion
  16.0 3.9 %reshape.123 = bf16[128,32,100]{2,1,0:T(8,128)(2,1)S(1)} reshape(bf16[128,3200]{1,0:T(8,128)(2,1)S(1)} %multiply_convert_fusion) | data formatting | bytes 1638400 | tf_op jit(solution)/shard_map/reshape | solution.py:576
  20.0 0.4 copy.37
  20.4 2.3 %maximum_bitcast_fusion.acts = bf16[32,128,256]{2,1,0:T(8,128)(2,1)} fusion(bf16[128,32,100]{2,0,1:T(8,128)(2,1)S(1)} %copy.37, bf16[128,32,100]{2,0,1:T(8,128)(2,1)S(1)} %copy.36, bf16[256]{0:T(256)(128)(2,1)S(1)} %pad.24.clone), kind=kLoop, calls=%fused_computation.2 | loop fusion | flops 6291456 | bytes 3736064 | tf_op jit(solution)/shard_map/transpose | solution.py:580
  22.7 103.5 %shard_map.102 = (f32[2,208,512]{2,1,0:T(8,128)}, f32[4,208,128]{2,1,0:T(8,128)}, bf16[2,16,448,128]{3,2,1,0:T(8,128)(2,1)}) custom-call(bf16[2,656,128]{2,1,0:T(8,128)(2,1)} %pad_maximum_fusion.1.wu, bf16[32,128,256]{2,1,0:T(8,128)(2,1)} %maximum_bitcast_fusion.acts, f32[4,112,128]{2,1,0:T(8,128)} %maximum_maximum_fusion.1.base, ...), custom_call_target="tpu_custom_call" | custom-call | tf_op jit(solution)/shard_map/pallas_call | solution.py:504
  126.2 0.8 multiply_bitcast_fusion
  126.9 0.9 slice.71
  127.9 0.8 fusion.7
  128.7 6.1 %copy.39 = bf16[2,16,448,128]{2,3,1,0:T(8,128)(2,1)} copy(bf16[2,16,448,128]{3,2,1,0:T(8,128)(2,1)} %get-tuple-element.8) | data formatting | bytes 7340032 | tf_op jit(solution)/shard_map/pallas_call | solution.py:504
  134.8 7.6 %reshape.107 = bf16[32,4,112,2,64]{2,1,4,3,0:T(4,128)(2,1)} reshape(bf16[2,16,448,128]{2,3,1,0:T(8,128)(2,1)} %copy.39) | data formatting | bytes 7340032 | tf_op jit(solution)/shard_map/reshape | solution.py:599
  142.4 2.1 %fusion.8 = s32[32,2]{1,0:T(8,128)S(1)} fusion(bf16[32,4,112,2,64]{2,1,4,3,0:T(4,128)(2,1)} %reshape.107), kind=kLoop, calls=%fused_computation.29 | loop fusion | flops 64 | bytes 384 | tf_op jit(solution)/shard_map/convert_element_type | solution.py:600
  144.5 0.1 reshape.112
  144.6 6.4 %slice_bitcast_fusion = bf16[32,2,4,100,64]{3,2,4,1,0:T(4,128)(2,1)} fusion(bf16[32,4,112,2,64]{2,1,4,3,0:T(4,128)(2,1)} %reshape.107), kind=kLoop, calls=%fused_computation.1 | loop fusion | bytes 6553600 | tf_op jit(solution)/shard_map/transpose | solution.py:606
  151.0 7.8 %reshape.108 = bf16[64,400,64]{1,2,0:T(8,128)(2,1)} reshape(bf16[32,2,4,100,64]{3,2,4,1,0:T(4,128)(2,1)} %slice_bitcast_fusion) | data formatting | bytes 6553600 | tf_op jit(solution)/shard_map/reshape | solution.py:606
  158.9 0.2 compare_reduce_fusion.1
  159.0 0.7 compare_reduce_fusion
  159.8 2.8 %gather_fusion = bf16[8,400,64]{1,2,0:T(8,128)(2,1)S(1)} fusion(bf16[64,400,64]{1,2,0:T(8,128)(2,1)} %reshape.108, s32[1024]{0:T(1024)S(1)} %pad_clamp_fusion), kind=kCustom, calls=%fused_computation | custom fusion | bytes 819232 | tf_op jit(solution)/shard_map/jit(_take)/gather | solution.py:607
  162.5 0.0 copy-start.2
  162.6 0.1 select_bitcast_fusion
  162.7 0.3 copy.40
  163.0 0.3 copy.41
  163.3 1.0 copy.43
  164.3 0.1 slice_bitcast_fusion.2
  164.4 0.9 maximum_bitcast_fusion.1
  165.2 0.9 pad_maximum_fusion
  (21 shorter events, 0.2 us)
Async XLA Ops:
  0.6 8.2 %copy-start.3 = (bf16[800,100]{0,1:T(8,128)(2,1)S(1)}, bf16[800,100]{0,1:T(8,128)(2,1)}, u32[]{:S(2)}) copy-start(bf16[800,100]{0,1:T(8,128)(2,1)} %param.12) | copy-start | bytes 480004
  0.6 8.2 %copy-start.4 = (bf16[100,800]{1,0:T(8,128)(2,1)S(1)}, bf16[100,800]{1,0:T(8,128)(2,1)}, u32[]{:S(2)}) copy-start(bf16[100,800]{1,0:T(8,128)(2,1)} %param.11) | copy-start | bytes 480004
  8.0 2.4 %copy-start = (bf16[128,3200]{1,0:T(8,128)(2,1)S(1)}, bf16[128,3200]{1,0:T(8,128)(2,1)}, u32[]{:S(2)}) copy-start(bf16[128,3200]{1,0:T(8,128)(2,1)} %param.7) | copy-start | bytes 2457604
  8.0 2.4 %copy-start.5 = (f32[3200]{0:T(1024)S(1)}, f32[3200]{0:T(1024)}, u32[]{:S(2)}) copy-start(f32[3200]{0:T(1024)} %param.9) | copy-start | bytes 38404
  10.6 4.4 %copy-start.6 = (f32[3200]{0:T(1024)S(1)}, f32[3200]{0:T(1024)}, u32[]{:S(2)}) copy-start(f32[3200]{0:T(1024)} %param.10) | copy-start | bytes 38404
  14.6 1.1 copy-start.1
  162.5 1.7 %copy-start.2 = (f32[2,208,512]{2,1,0:T(8,128)S(1)}, f32[2,208,512]{2,1,0:T(8,128)}, u32[]{:S(2)}) copy-start(f32[2,208,512]{2,1,0:T(8,128)} %get-tuple-element.11) | copy-start | bytes 2555908

commit v2 on v1

v2 whole, which is shorter than its diff:
```python
import jax
import jax.numpy as jnp
from jax import lax
from jax.experimental import pallas as pl
from jax.experimental.pallas import tpu as pltpu
from jax.sharding import PartitionSpec as P

BLK = 8
FE = 100
HH = 400
UR = 208
PK = 656
HA = 336
PARTS = ((0, HA), (HA, PK - HA))
MESH = pl.DeviceIdType.MESH
F32 = jnp.float32
BF = jnp.bfloat16


def fold_tail(tail):
    tail = jnp.concatenate([tail, jnp.zeros((16, 128), F32)], axis=0)
    out = tail[0:32]
    for g in range(1, 7):
        out = out + pltpu.roll(tail[32 * g : 32 * g + 32], 16 * g, 1)
    return out


def unfold_tail(packed):
    packed = packed.astype(F32)
    rows = [packed] + [pltpu.roll(packed, 128 - 16 * g, 1) for g in range(1, 7)]
    return jnp.concatenate(rows, axis=0)[:UR]


def kernel(
    wu, vec, live, patches, upstream, g_out, gp_out, tab_out, v_out,
    xin, uin, nsc, gsc, rsc, RM, U, C2, X2, CT, hacc, S, ST, PG, rb1, rb2, ra1, ra2, fin, M, MR, zrm, zrp, V, cen,
    ag_s, ag_r, rs_s, rs_r, vg_s, vg_r, vf_s, vf_r, sq_s, sq_r, zz_s, zz_r, mi_s, mi_r, loc,
):
    dp = lax.axis_index("dp")
    z = lax.axis_index("mp")
    c = lax.rem(dp, 2)
    x = lax.rem(dp // 2, 4)
    y = dp // 8
    me = y * 4 + x
    UU = (0, 1)

    def chip_of(u, da, db):
        if u == 0:
            return lax.rem(y + db, 4) * 4 + lax.rem(x + da, 4)
        return lax.rem(y + da, 4) * 4 + lax.rem(x + db, 4)

    def dev(u, da, db):
        return (chip_of(u, da, db) * 2 + c, z)

    def zdev(dz):
        return (dp, lax.rem(z + dz, 8))

    sib = (me * 2 + 1 - c, z)
    ap = [dev(u, 1, 0) for u in UU]
    am = [dev(u, 3, 0) for u in UU]
    bp = [dev(u, 0, 1) for u in UU]
    bm = [dev(u, 0, 3) for u in UU]
    nbrs = [sib, ap[0], am[0], bp[0], bm[0], zdev(1), zdev(7)]

    def rc(src, dst, ss, rs, d):
        return pltpu.make_async_remote_copy(
            src_ref=src, dst_ref=dst, send_sem=ss, recv_sem=rs, device_id=d, device_id_type=MESH
        )

    def uidx(u, da, db):
        return chip_of(u, da, db) * 2 + (c if u == 0 else 1 - c)

    def da_of(k):
        return k + k // 2 - 2 * (k // 3)

    get_p = pltpu.make_async_copy(patches, xin, loc.at[1])
    get_u = pltpu.make_async_copy(upstream, uin, loc.at[2])
    own = pltpu.make_async_copy(wu.at[c], U.at[me * 2 + c], loc.at[0])
    own.start()
    get_p.start()
    get_u.start()
    barrier = pltpu.get_barrier_semaphore()
    for d in nbrs:
        pl.semaphore_signal(barrier, inc=1, device_id=d, device_id_type=MESH)
    pl.semaphore_wait(barrier, len(nbrs))

    class Gather:
        def __init__(self, slot, ss, rs):
            self.slot, self.ss, self.rs = slot, ss, rs

        def copy(self, u, m, p, da, db, d):
            ref = self.slot(u, p, da, db)
            return rc(ref, ref, self.ss.at[u, m, p], self.rs.at[u, m, p], d)

        def send(self, u, m, p, da, db, d):
            self.copy(u, m, p, da, db, d).start()

        def wait(self, u, m, p, da, db):
            self.copy(u, m, p, da, db, sib).wait_recv()

        def bsend(self, u, k, p):
            da = da_of(k)
            self.send(u, 3 + 3 * k, p, da, 0, bp[u])
            self.send(u, 4 + 3 * k, p, da, 0, bm[u])

        def start_a(self, u):
            self.send(u, 0, 0, 0, 0, ap[u])
            self.send(u, 1, 1, 0, 0, am[u])
            self.send(u, 0, 1, 0, 0, ap[u])
            self.send(u, 1, 0, 0, 0, am[u])

        def start_b(self, u):
            self.send(u, 3, 0, 0, 0, bp[u])
            self.send(u, 4, 1, 0, 0, bm[u])
            self.send(u, 3, 1, 0, 0, bp[u])
            self.send(u, 4, 0, 0, 0, bm[u])

        def near0(self, u):
            self.wait(u, 0, 0, 3, 0)
            self.send(u, 2, 0, 3, 0, ap[u])
            self.wait(u, 1, 1, 1, 0)
            self.send(u, 2, 1, 1, 0, am[u])
            self.bsend(u, 2, 0)
            self.bsend(u, 1, 1)

        def near1(self, u):
            self.wait(u, 0, 1, 3, 0)
            self.bsend(u, 2, 1)
            self.wait(u, 1, 0, 1, 0)
            self.bsend(u, 1, 0)

        def far(self, u):
            self.wait(u, 2, 0, 2, 0)
            self.bsend(u, 3, 0)
            self.wait(u, 2, 1, 2, 0)
            self.bsend(u, 3, 1)

        def bfwd(self, u, k):
            da = da_of(k)
            self.wait(u, 3 + 3 * k, 0, da, 3)
            self.send(u, 5 + 3 * k, 0, da, 3, bp[u])
            self.wait(u, 4 + 3 * k, 1, da, 1)
            self.send(u, 5 + 3 * k, 1, da, 1, bm[u])

        def brest(self, u, k):
            da = da_of(k)
            self.wait(u, 3 + 3 * k, 1, da, 3)
            self.wait(u, 4 + 3 * k, 0, da, 1)

        def blast(self, u, k):
            da = da_of(k)
            self.wait(u, 5 + 3 * k, 0, da, 2)
            self.wait(u, 5 + 3 * k, 1, da, 2)

        def done(self):
            def body(m, carry):
                for u in UU:
                    for p in (0, 1):
                        self.copy(u, m, p, 0, 0, sib).wait_send()
                return carry

            lax.fori_loop(0, 15, body, 0)

    def wslot(u, p, da, db):
        return U.at[uidx(u, da, db), pl.ds(*PARTS[p])]

    ag = Gather(wslot, ag_s, ag_r)

    to_sib = rc(wu.at[1 - c], U.at[me * 2 + c], mi_s.at[0], mi_r.at[0], sib)
    to_sib.start()
    own.wait()
    ag.start_a(0)
    rc(wu.at[0], U.at[me * 2 + 1 - c], mi_s.at[0], mi_r.at[0], sib).wait_recv()
    ag.start_a(1)
    ag.start_b(0)
    ag.start_b(1)

    hacc[...] = jnp.zeros_like(hacc)
    get_p.wait()
    get_u.wait()

    def act_step(r, carry):
        r0 = pl.multiple_of(r * 16, 16)
        xs = xin[pl.ds(r0, 16), :].astype(F32)
        root = jnp.sqrt(jnp.sum(xs * xs, axis=1, keepdims=True) * (1.0 / 3200.0) + 1e-06)
        RM[pl.ds(r0, 16), :] = jnp.broadcast_to(root, (16, 128))
        up_live = uin[pl.ds(r0, 16), :].astype(F32) * live[pl.ds(r0, 16), 0:1]
        nsc[...] = xs / root * vec[0:1, :]
        gsc[...] = up_live * vec[1:2, :]
        rsc[0] = up_live
        rsc[1] = xs
        lane = lax.broadcasted_iota(jnp.int32, (16, 256), 1)
        for i in range(32):
            q = min(100 * i // 128, 23)
            sh = 100 * i - 128 * q
            win = slice(128 * q, 128 * q + 256)

            def pair(a, b):
                a = pltpu.roll(a, (256 - sh) % 256, 1)
                b = pltpu.roll(b, (100 - sh) % 256, 1)
                return jnp.where(lane < FE, a, jnp.where(lane < 2 * FE, b, 0.0)).astype(BF)

            C2[c, i, pl.ds(r0, 16), :] = pair(nsc[:, win], gsc[:, win])
            X2[i, pl.ds(r0, 16), :] = pair(rsc[0, :, win], rsc[1, :, win])
        return carry

    lax.fori_loop(0, 8, act_step, 0)
    act_sib = rc(C2.at[c], C2.at[c], mi_s.at[1], mi_r.at[1], sib)
    act_sib.start()

    def weight(i):
        w = U[i]
        tail = unfold_tail(w[624:656]).astype(BF)
        return jnp.concatenate([w[0:208], w[208:416], w[416:624], tail], axis=1)

    def up(i):
        act = jnp.concatenate([C2[0, i], C2[1, i]], axis=0)
        CT[i] = act.T[:UR]
        a = act[:, :UR]
        first = lax.broadcasted_iota(jnp.int32, a.shape, 1) < FE
        zero = jnp.zeros_like(a)
        lhs = jnp.concatenate([jnp.where(first, a, zero), jnp.where(first, zero, a)], axis=0)
        hacc[...] += jnp.dot(lhs, weight(i), preferred_element_type=F32)

    def up_all(units):
        for u, da, db in units:
            up(uidx(u, da, db))

    for u in UU:
        ag.near0(u)
    for u in UU:
        ag.near1(u)
    rc(C2.at[c], C2.at[1 - c], mi_s.at[1], mi_r.at[1], sib).wait_recv()
    for u in UU:
        ag.bfwd(u, 0)
    up_all([(0, 0, 0), (1, 0, 0)])
    for u in UU:
        ag.far(u)
    up_all([(u, da, 0) for u in UU for da in (3, 1)])

    def fwd_step(k, carry):
        for u in UU:
            ag.bfwd(u, k)
        for u in UU:
            ag.brest(u, k - 1)
        up_all([(u, da_of(k - 1), db) for u in UU for db in (3, 1)])
        return carry

    lax.fori_loop(1, 4, fwd_step, 0)
    up_all([(0, 2, 0), (1, 2, 0)])

    def last_step(k, carry):
        for u in UU:
            ag.blast(u, k)
        up_all([(u, da_of(k), 2) for u in UU])
        return carry

    lax.fori_loop(0, 3, last_step, 0)
    for u in UU:
        ag.brest(u, 3)
    up_all([(u, da_of(3), db) for u in UU for db in (3, 1)])
    last_step(3, 0)

    def gelu_step(r, carry):
        r0 = pl.multiple_of(r * 32, 32)
        h = hacc[pl.ds(r0, 32), :]
        gh = hacc[pl.ds(r0 + 256, 32), :]
        valid = lax.broadcasted_iota(jnp.int32, h.shape, 1) < HH
        cumul = 0.5 * (1.0 + lax.erf(h * 0.7071067811865476))
        density = jnp.exp(-0.5 * h * h) * 0.3989422804014327
        ho = jnp.where(valid, h * cumul, 0.0).astype(BF)
        gi = jnp.where(valid, gh * (cumul + h * density), 0.0).astype(BF)
        S[pl.ds(r0, 32), :] = gi
        S[pl.ds(r0 + 256, 32), :] = ho
        row = jnp.sum(gi.astype(F32) * jnp.where(valid, h, 0.0), axis=1, keepdims=True)
        cen[pl.ds(r0, 32), :] = jnp.broadcast_to(row, (32, 128))
        return carry

    lax.fori_loop(0, 8, gelu_step, 0)

    def down(i):
        ct = CT[i]
        first = lax.broadcasted_iota(jnp.int32, ct.shape, 0) < FE
        zero = jnp.zeros_like(ct)
        lhs = jnp.concatenate([jnp.where(first, ct, zero), jnp.where(first, zero, ct)], axis=1)
        out = jnp.dot(lhs, S[...], preferred_element_type=F32)
        return [out[:, 0:128], out[:, 128:256], out[:, 256:384], fold_tail(out[:, 384:512])]

    ROWS4 = ((0, 208), (208, 416), (416, 624), (624, 656))

    def store_unit(i, *adds):
        for (lo, hi), part in zip(ROWS4, down(i)):
            for ref in adds:
                part = part + ref[lo:hi].astype(F32)
            PG[i, lo:hi] = part.astype(BF)

    def add_part(i, p, ref):
        lo, n = PARTS[p]
        PG[i, lo : lo + n] = (PG[i, lo : lo + n].astype(F32) + ref[lo : lo + n].astype(F32)).astype(BF)

    def rs(u, m, p, i, buf, d):
        return rc(
            PG.at[i, pl.ds(*PARTS[p])], buf.at[pl.ds(*PARTS[p])], rs_s.at[u, m, p], rs_r.at[u, m, p], d
        )

    def rs_wait(u, m, p, buf):
        rs(u, m, p, 0, buf, sib).wait_recv()

    def first_down(kk, carry):
        k = 3 - kk
        for u in UU:
            i = uidx(u, da_of(k), 2)
            store_unit(i)
            rs(u, 3 + 3 * k, 0, i, rb1.at[u, k], bp[u]).start()
            rs(u, 3 + 3 * k, 1, i, rb1.at[u, k], bm[u]).start()
        return carry

    lax.fori_loop(0, 4, first_down, 0)
    ST[...] = S[...].T
    center = cen[...].T[0:1]
    cen_hi = center.astype(BF).astype(F32)
    cen_lo = center - cen_hi

    def zblk(r):
        return lax.rem(z + r, 8)

    def mix(b):
        def body(j, carry):
            i = b * 4 + j
            out = jnp.dot(weight(i), ST[...], preferred_element_type=F32)
            row = lax.broadcasted_iota(jnp.int32, (UR, 256), 0)
            m = jnp.where(row < FE, out[:, :256], out[:, 256:])
            m = jnp.where(row == 200, cen_hi, jnp.where(row == 201, cen_lo, m)).astype(BF)
            M[0, i] = m[:, :128]
            M[1, i] = m[:, 128:]
            return carry

        lax.fori_loop(0, 4, body, 0)

    def to_sibling(s, r):
        b = zblk(r)
        return rc(M.at[1 - c, pl.ds(4 * b, 4)], MR.at[pl.ds(4 * b, 4)], sq_s.at[s], sq_r.at[s], sib)

    zorder = (4, 3, 5, 2, 6, 1, 7, 0)

    def mix_step(s, carry):
        h = (s + 1) // 2
        r = 4 + h - 2 * h * lax.rem(s, 2)
        mix(zblk(r))
        to_sibling(s, r).start()
        return carry

    def zcopy(way, j, h):
        r = 4 + j if way == 0 else 4 - j
        buf = zrm if way == 0 else zrp
        return rc(
            M.at[c, pl.ds(4 * zblk(r) + 2 * h, 2)], buf.at[j, pl.ds(2 * h, 2)],
            zz_s.at[way, j, h], zz_r.at[way, j, h], zdev(7 if way == 0 else 1),
        )

    def combine(r, h, ref):
        b = zblk(r)
        for j in (2 * h, 2 * h + 1):
            i = b * 4 + j
            t = M[c, i].astype(F32) + MR[i].astype(F32)
            if ref is not None:
                t = t + ref[j].astype(F32)
            M[c, i] = t.astype(BF)

    def zfirst():
        to_sibling(0, 4).wait_recv()
        for way in (0, 1):
            combine(4, way, None)
            zcopy(way, 0, way).start()

    def zstep(j):
        for h in ((1, 0) if j == 1 else (0, 1)):
            for way in (0, 1):
                buf = zrm if way == 0 else zrp
                r = 4 + j if way == 0 else 4 - j
                if h == 1 if j == 1 else h == 0:
                    to_sibling(2 * j if way == 0 else 2 * j - 1, r).wait_recv()
                hh = h if way == 0 or j > 1 else 1 - h
                if j == 1 and hh != way:
                    combine(r, hh, None)
                else:
                    zcopy(way, j - 1, hh).wait_recv()
                    combine(r, hh, buf.at[j - 1])
                zcopy(way, j, hh).start()

    lax.fori_loop(0, 4, mix_step, 0)
    zfirst()
    lax.fori_loop(4, 8, mix_step, 0)

    def second_down(kk, carry):
        k = 3 - kk
        for u in UU:
            i = uidx(u, da_of(k), 1)
            store_unit(i)
            rs(u, 4 + 3 * k, 1, i, rb2.at[u, 0, k], bp[u]).start()
            i = uidx(u, da_of(k), 3)
            store_unit(i)
            rs(u, 5 + 3 * k, 0, i, rb2.at[u, 1, k], bm[u]).start()
        for u in UU:
            i = uidx(u, da_of(k), 1)
            rs_wait(u, 3 + 3 * k, 0, rb1.at[u, k])
            add_part(i, 0, rb1.at[u, k])
            rs(u, 4 + 3 * k, 0, i, rb2.at[u, 0, k], bp[u]).start()
            i = uidx(u, da_of(k), 3)
            rs_wait(u, 3 + 3 * k, 1, rb1.at[u, k])
            add_part(i, 1, rb1.at[u, k])
            rs(u, 5 + 3 * k, 1, i, rb2.at[u, 1, k], bm[u]).start()
        return carry

    lax.fori_loop(0, 2, second_down, 0)
    zstep(1)
    lax.fori_loop(2, 4, second_down, 0)
    zstep(2)

    def third(u, k):
        for w in (0, 1):
            for p in (1, 0) if w == 0 else (0, 1):
                rs_wait(u, 4 + 3 * k + w, p, rb2.at[u, w, k])
        i = uidx(u, da_of(k), 0)
        store_unit(i, rb2.at[u, 0, k], rb2.at[u, 1, k])
        return i

    for u in UU:
        i = third(u, 3)
        rs(u, 0, 0, i, ra1.at[u], ap[u]).start()
        rs(u, 0, 1, i, ra1.at[u], am[u]).start()
    for u in UU:
        i = third(u, 1)
        rs(u, 1, 1, i, ra2.at[u, 0], ap[u]).start()
        i = third(u, 2)
        rs(u, 2, 0, i, ra2.at[u, 1], am[u]).start()
    zstep(3)
    for u in UU:
        rs_wait(u, 0, 0, ra1.at[u])
        i = uidx(u, 1, 0)
        add_part(i, 0, ra1.at[u])
        rs(u, 1, 0, i, ra2.at[u, 0], ap[u]).start()
        rs_wait(u, 0, 1, ra1.at[u])
        i = uidx(u, 3, 0)
        add_part(i, 1, ra1.at[u])
        rs(u, 2, 1, i, ra2.at[u, 1], am[u]).start()

    to_sibling(7, 0).wait_recv()
    for h in (0, 1):
        for way in (0, 1):
            zcopy(way, 3, h).wait_recv()
    root = RM[:, 0:1]
    lane = lax.broadcasted_iota(jnp.int32, (128, 256), 1)
    centre = None
    res = []
    for j in range(4):
        i = z * 4 + j
        t = M[c, i].astype(F32) + MR[i].astype(F32) + zrm[3, j].astype(F32) + zrp[3, j].astype(F32)
        t = jnp.concatenate([t, jnp.zeros((256 - UR, 128), F32)], axis=0).T
        if j == 0:
            centre = (t[:, 200:201] + t[:, 201:202]) * (1.0 / 3200.0)
        raw = X2[i].astype(F32)
        gains = vec_units(vec, i)
        moved = pltpu.roll(raw, 156, 1)
        gp = raw + (gains * t - moved / root * centre) / root
        gp_out[j] = gp[:, :128].astype(BF)
        res.append(pltpu.roll(raw + gains * t, 156, 1)[:, :128])
    out = jnp.where(lane[:, :128] < FE, res[0], 0.0)
    wide = [out, jnp.zeros_like(out), jnp.zeros_like(out), jnp.zeros_like(out)]
    for j in (1, 2, 3):
        at, sh = divmod(FE * j, 128)
        r = pltpu.roll(res[j], sh, 1)
        ln = lane[:, :128]
        first = (ln >= sh) & (ln < sh + FE)
        wide[at] = jnp.where(first, r, wide[at])
        if sh + FE > 128:
            wide[at + 1] = jnp.where(ln < sh + FE - 128, r, wide[at + 1])
    tail = jnp.where(lane[:, :128] < 16, wide[3], 0.0)
    folded = tail[0:16]
    for g in range(1, 8):
        folded = folded + pltpu.roll(tail[16 * g : 16 * g + 16], 16 * g, 1)
    for t in range(3):
        V[c, me, 128 * t : 128 * t + 128, :] = wide[t].astype(BF)
    V[c, me, 384:400, :] = folded.astype(BF)

    VP = (((0, 112), (112, 96)), ((208, 96), (304, 96)))

    def vslot(u, p, da, db):
        return V.at[c, chip_of(u, da, db), pl.ds(*VP[u][p])]

    vg = Gather(vslot, vg_s, vg_r)

    def fwd(u, da, db):
        ch = chip_of(u, da, db)
        ref = V.at[c, ch, pl.ds(208 * u, 208 - 16 * u)]
        return rc(ref, ref, vf_s.at[u, ch], vf_r.at[u, ch], sib)

    for u in UU:
        vg.start_a(u)
    for u in UU:
        vg.start_b(u)
    for u in UU:
        fwd(u, 0, 0).start()

    def finish(u):
        for w in (0, 1):
            for p in (1, 0) if w == 0 else (0, 1):
                rs_wait(u, 4 + w, p, rb2.at[u, w, 0])
        i = uidx(u, 0, 0)
        parts = down(i)
        for w in (0, 1):
            for p in (1, 0) if w == 0 else (0, 1):
                rs_wait(u, 1 + w, p, ra2.at[u, w])
        out = []
        for (lo, hi), part in zip(ROWS4, parts):
            for ref in (rb2.at[u, 0, 0], rb2.at[u, 1, 0], ra2.at[u, 0], ra2.at[u, 1]):
                part = part + ref[lo:hi].astype(F32)
            out.append(part)
        return i, out

    i, parts = finish(1)
    for (lo, hi), part in zip(ROWS4, parts):
        PG[i, lo:hi] = part.astype(BF)
    to_fin = rc(PG.at[i], fin, mi_s.at[2], mi_r.at[2], sib)
    to_fin.start()
    for u in UU:
        vg.near0(u)
    for u in UU:
        vg.near1(u)
    _, parts = finish(0)
    for t in range(3):
        g_out[c, :, 128 * t : 128 * t + 128] = parts[t]
    g_out[c, :, 384:512] = unfold_tail(parts[3])

    for u in UU:
        fwd(u, 3, 0).start()
        fwd(u, 1, 0).start()
    for u in UU:
        vg.bfwd(u, 0)
    for u in UU:
        vg.far(u)
        fwd(u, 2, 0).start()

    def vstep(k, carry):
        for u in UU:
            vg.bfwd(u, k)
        for u in UU:
            vg.brest(u, k - 1)
            fwd(u, da_of(k - 1), 3).start()
            fwd(u, da_of(k - 1), 1).start()
        return carry

    lax.fori_loop(1, 4, vstep, 0)

    to_fin.wait_recv()
    for t in range(3):
        g_out[1 - c, :, 128 * t : 128 * t + 128] = fin[208 * t : 208 * t + 208].astype(F32)
    g_out[1 - c, :, 384:512] = unfold_tail(fin[624:656])
    tab_out[...] = U[:, 192:208, :].astype(F32)[:, 8, :]

    for u in UU:
        vg.brest(u, 3)
        fwd(u, 2, 3).start()
        fwd(u, 2, 1).start()

    def vlast(k, carry):
        for u in UU:
            vg.blast(u, k)
            fwd(u, da_of(k), 2).start()
        return carry

    lax.fori_loop(0, 4, vlast, 0)

    def vfwd_wait(ch, carry):
        for u in UU:
            ref = V.at[1 - c, ch, pl.ds(208 * u, 208 - 16 * u)]
            d = rc(ref, ref, vf_s.at[u, ch], vf_r.at[u, ch], sib)
            d.wait_recv()
            d.wait_send()
        return carry

    lax.fori_loop(0, 16, vfwd_wait, 0)
    vcopy = pltpu.make_async_copy(V, v_out, loc.at[3])
    vcopy.start()

    ag.done()
    vg.done()
    to_sib.wait_send()
    act_sib.wait_send()
    to_fin.wait_send()
    for s in range(8):
        to_sibling(s, zorder[s]).wait_send()
    for way in (0, 1):
        zcopy(way, 0, way).wait_send()
        for j in (1, 2, 3):
            for h in (0, 1):
                zcopy(way, j, h).wait_send()

    def rs_done(m, carry):
        for u in UU:
            for p in (0, 1):
                rs(u, m, p, 0, ra1.at[u], sib).wait_send()
        return carry

    lax.fori_loop(0, 15, rs_done, 0)
    vcopy.wait()


def vec_units(vec, i):
    return vec[pl.ds(2 + i, 1), 0:256]


def mega(wu, vec, live, patches, upstream):
    dma = pltpu.SemaphoreType.DMA
    vm = pl.BlockSpec(memory_space=pltpu.VMEM)
    hbm = pl.BlockSpec(memory_space=pl.ANY)
    return pl.pallas_call(
        kernel,
        out_shape=(
            jax.ShapeDtypeStruct((2, UR, 512), F32),
            jax.ShapeDtypeStruct((4, 128, 128), BF),
            jax.ShapeDtypeStruct((32, 128), F32),
            jax.ShapeDtypeStruct((2, 16, 400, 128), BF),
        ),
        in_specs=[vm, vm, vm, hbm, hbm],
        out_specs=(vm, vm, vm, hbm),
        scratch_shapes=[
            pltpu.VMEM((128, 3200), BF),
            pltpu.VMEM((128, 3200), BF),
            pltpu.VMEM((16, 3200), F32),
            pltpu.VMEM((16, 3200), F32),
            pltpu.VMEM((2, 16, 3200), F32),
            pltpu.VMEM((128, 128), F32),
            pltpu.VMEM((32, PK, 128), BF),
            pltpu.VMEM((2, 32, 128, 256), BF),
            pltpu.VMEM((32, 128, 256), BF),
            pltpu.VMEM((32, UR, 256), BF),
            pltpu.VMEM((512, 512), F32),
            pltpu.VMEM((512, 512), BF),
            pltpu.VMEM((512, 512), BF),
            pltpu.VMEM((32, PK, 128), BF),
            pltpu.VMEM((2, 4, PK, 128), BF),
            pltpu.VMEM((2, 2, 4, PK, 128), BF),
            pltpu.VMEM((2, PK, 128), BF),
            pltpu.VMEM((2, 2, PK, 128), BF),
            pltpu.VMEM((PK, 128), BF),
            pltpu.VMEM((2, 32, UR, 128), BF),
            pltpu.VMEM((32, UR, 128), BF),
            pltpu.VMEM((4, 4, UR, 128), BF),
            pltpu.VMEM((4, 4, UR, 128), BF),
            pltpu.VMEM((2, 16, 400, 128), BF),
            pltpu.VMEM((256, 128), F32),
            dma((2, 15, 2)), dma((2, 15, 2)),
            dma((2, 15, 2)), dma((2, 15, 2)),
            dma((2, 15, 2)), dma((2, 15, 2)),
            dma((2, 16)), dma((2, 16)),
            dma((8,)), dma((8,)),
            dma((2, 4, 2)), dma((2, 4, 2)),
            dma((3,)), dma((3,)),
            dma((4,)),
        ],
        compiler_params=pltpu.CompilerParams(
            collective_id=0, has_side_effects=True, vmem_limit_bytes=60 * 2**20
        ),
    )(wu, vec, live, patches, upstream)


def finish_kernel(g, gp, tab, v, w_in_out, w_out_out, gp_out, vis_out, tiles, sem):
    first = lax.axis_index("dp") * BLK
    table = tab[...]
    row = lax.broadcasted_iota(jnp.int32, table.shape, 0)
    lane = lax.broadcasted_iota(jnp.int32, table.shape, 1)
    code = (2 * row + lane).astype(F32)
    which = []
    copies = []
    for b in range(BLK):
        hit = (table == (first + b).astype(F32)) & (lane < 2)
        at = jnp.max(jnp.where(hit, code, -1.0)).astype(jnp.int32)
        which.append(at)
        dev = jnp.maximum(at, 0) // 2
        copy = pltpu.make_async_copy(v.at[lax.rem(dev, 2), dev // 2], tiles.at[b], sem.at[b])
        copy.start()
        copies.append(copy)
    for h in (0, 1):
        w_in_out[:, HH * h : HH * h + HH] = g[h, 0:FE, 0:HH]
        w_out_out[HH * h : HH * h + HH, :] = g[h, FE : 2 * FE, 0:HH].T
    for j in range(4):
        gp_out[:, FE * j : FE * j + FE] = gp[j, :, 0:FE]
    to = lax.broadcasted_iota(jnp.int32, (64, 64), 0)
    fr = lax.broadcasted_iota(jnp.int32, (64, 64), 1)
    perm = (fr == 32 * (lax.rem(to, 4) // 2) + 2 * (to // 4) + lax.rem(to, 2)).astype(BF)
    for b in range(BLK):
        copies[b].wait()
        at = which[b]
        odd = lax.rem(at, 2) == 1
        parts = []
        for t in range(3):
            lo = tiles[b, 128 * t : 128 * t + 64]
            hi = tiles[b, 128 * t + 64 : 128 * t + 128]
            parts.append(jnp.where(odd, hi, lo))
        tail = tiles[b, 384:400].astype(F32)
        tail = jnp.where(odd, pltpu.roll(tail, 64, 1), tail)
        tail = [tail] + [pltpu.roll(tail, 128 - 16 * g, 1) for g in (1, 2, 3)]
        parts.append(jnp.concatenate(tail, axis=0).astype(BF))
        tile = jnp.concatenate(parts, axis=1)
        out = jnp.dot(perm, tile, preferred_element_type=F32)
        out = jnp.where(at >= 0, out, 0.0).astype(BF)
        vis_out[64 * b : 64 * b + 64, :] = out[:, 0:HH]


def finish(g, gp, tab, v):
    vm = pl.BlockSpec(memory_space=pltpu.VMEM)
    return pl.pallas_call(
        finish_kernel,
        out_shape=(
            jax.ShapeDtypeStruct((FE, 2 * HH), F32),
            jax.ShapeDtypeStruct((2 * HH, FE), F32),
            jax.ShapeDtypeStruct((128, HH), BF),
            jax.ShapeDtypeStruct((BLK * 64, HH), BF),
        ),
        in_specs=[vm, vm, vm, pl.BlockSpec(memory_space=pl.ANY)],
        out_specs=(vm, vm, vm, vm),
        scratch_shapes=[pltpu.VMEM((BLK, 400, 128), BF), pltpu.SemaphoreType.DMA((BLK,))],
        compiler_params=pltpu.CompilerParams(vmem_limit_bytes=32 * 2**20),
    )(g, gp, tab, v)


def pack_units(w_in, w_out, slot_block):
    table = jnp.pad(slot_block.astype(BF)[None, :], ((0, 7), (0, 2 * HH - 2)))
    table = table + jnp.roll(table, HH, axis=1)
    both = jnp.concatenate([w_in, w_out.T, table], axis=0)
    halves = []
    for h in (0, 1):
        part = both[:, HH * h : HH * h + HH]
        tail = jnp.pad(part[:, 384:], ((0, 48), (0, 0)))
        tail = tail.reshape(8, 32, 16).transpose(1, 0, 2).reshape(32, 128)
        halves.append(
            jnp.concatenate([part[:, 0:128], part[:, 128:256], part[:, 256:384], tail], axis=0)
        )
    return jnp.stack(halves)


def shards(patches, upstream, norm_gain, layer_scale, w_in, w_out, slot_block):
    rows = patches.shape[0]
    wu = pack_units(w_in, w_out, slot_block)
    live = jnp.repeat((slot_block >= 0).astype(F32), rows // 2)[:, None]
    live = jnp.broadcast_to(live, (rows, 128))
    units = jnp.concatenate([norm_gain.reshape(32, FE), layer_scale.reshape(32, FE)], axis=1)
    units = jnp.pad(units, ((0, 0), (0, 3200 - 2 * FE)))
    vec = jnp.concatenate([norm_gain[None], layer_scale[None], units], axis=0)
    g, gp, tab, v = mega(wu, vec, live, patches, upstream)
    grad_w_in, grad_w_out, grad_patches, vision = finish(g, gp, tab, v)
    return (vision.reshape(BLK * 16, 4, HH), grad_patches, grad_w_in, grad_w_out)


def solution(mesh):
    return jax.shard_map(
        shards,
        mesh=mesh,
        in_specs=(P("dp", None), P("dp", None), P(), P(), P("dp", "mp"), P("mp", "dp"), P("dp")),
        out_specs=(P("dp", None, "mp"), P("dp", "mp"), P("dp", "mp"), P("mp", "dp")),
        check_vma=False,
    )
```

time: 167 us -> 122 us (0.73)
  local copies, waits for them, and re-layouts: 48 us -> 12.2 us
  other arithmetic: 13.8 us -> 4.27 us
    reshape x9 -> x3, local copies, waits for them, and re-layouts: 24.3 us -> 1.78 us  [the longest x1 0.82 us: shards(): norm_gain.reshape(32, FE)]
    transpose x2 -> x0, local copies, waits for them, and re-layouts: 6.69 us -> none  [the longest x1 6.4 us: shards(): flat = tiles[:, :, 4:104].transpose(0, 3, 1, 2, 4).reshape(64, share, 64)]
    pallas_call x1 -> x0, local copies, waits for them, and re-layouts: 6.1 us -> none  [mega(): pl.pallas_call(kernel, out_shape=(jax.ShapeDtypeStruct((2, UR, 512), F32)...]
    unnamed x17 -> x11, local copies, waits for them, and re-layouts: 1.95 us -> 7.53 us
    pallas_call x0 -> x1, Pallas kernels: none -> 5.22 us  [finish(): pl.pallas_call(finish_kernel, out_shape=(jax.ShapeDtypeStruct((FE, 2 * HH...]
    pallas_call x1, Pallas kernels: 103 us -> 99.1 us  [mega(): pl.pallas_call(kernel, out_shape=(jax.ShapeDtypeStruct((2, UR, 512), F32)...]
    convert_element_type x6 -> x1, other arithmetic: 4.77 us -> 0.66 us  [shards(): live = jnp.repeat((slot_block >= 0).astype(F32), rows // 2)[:, None]]
    transpose x3 -> x0, other arithmetic: 3.22 us -> none  [the longest x1 2.34 us: shards(): acts = jnp.concatenate([normed.reshape(rows, 32, FE), grad_mixed.reshape(...]
where the time goes in v2:
time: 122 us
  Pallas kernels  104 us (85%)
  local copies, waits for them, and re-layouts  12.2 us (10%)
  other arithmetic  4.27 us (3%)
    pallas_call x1, Pallas kernels, mega(): pl.pallas_call(kernel, out_shape=(jax.ShapeDtypeStruct((2, UR, 512), F32)...  99.1 us
    unnamed x11, local copies, waits for them, and re-layouts  7.53 us
    pallas_call x1, Pallas kernels, finish(): pl.pallas_call(finish_kernel, out_shape=(jax.ShapeDtypeStruct((FE, 2 * HH...  5.22 us

profile of v2, /device:TPU:1, one launch (start us, length us, event | category | flops | bytes accessed | tf_op | source)
XLA Modules:
  0.0 121.6 jit_solution(3954601671044992954)
XLA Ops:
  0.6 0.7 convert_bitcast_fusion
  1.3 0.7 compare_convert_fusion
  1.9 0.1 broadcast_in_dim.22
  2.0 0.1 broadcast_in_dim.23
  2.1 0.1 pad_add_fusion
  2.2 0.7 broadcast_in_dim.20
  2.9 0.7 broadcast_in_dim.21
  3.7 0.8 reshape.34
  4.5 0.8 reshape.35
  5.3 0.7 broadcast_in_dim.24.live
  6.0 1.1 pad_maximum_fusion.1
  7.1 0.1 fusion.1
  7.2 0.1 fusion
  7.3 0.1 copy.16
  7.4 0.1 copy.17
  7.5 0.1 copy.18
  7.6 0.1 copy.19
  7.7 0.1 maximum_bitcast_fusion
  7.8 0.8 pad_maximum_fusion.2.wu
  8.5 0.1 select_maximum_fusion
  8.6 0.9 pad_maximum_fusion.vec
  9.5 99.1 %shard_map.102 = (f32[2,208,512]{2,1,0:T(8,128)}, bf16[4,128,128]{2,1,0:T(8,128)(2,1)}, f32[32,128]{1,0:T(8,128)}, bf16[2,16,400,128]{3,2,1,0:T(8,128)(2,1)}) custom-call(bf16[2,656,128]{2,1,0:T(8,128)(2,1)} %pad_maximum_fusion.2.wu, f32[34,3200]{1,0:T(8,128)} %pad_maximum_fusion.vec, f32[128,128]{1,0:T(8,128)} %broadcast_in_dim.24.live, ...), custom_call_target="tpu_custom_call" | custom-call | tf_op jit(solution)/shard_map/pallas_call | solution.py:617
  108.6 0.0 copy-start
  108.6 1.9 %copy-done = bf16[2,16,400,128]{3,2,1,0:T(8,128)(2,1)S(1)} copy-done((bf16[2,16,400,128]{3,2,1,0:T(8,128)(2,1)S(1)}, bf16[2,16,400,128]{3,2,1,0:T(8,128)(2,1)}, u32[]{:S(2)}) %copy-start) | copy-done | bytes 3276824
  110.6 0.0 copy-start.1
  110.6 1.2 copy-done.1
  111.7 0.0 copy-start.2
  111.7 0.9 copy-done.2
  112.6 0.0 copy-start.3
  112.6 0.7 copy-done.3
  113.3 5.2 %shard_map.103 = (f32[100,800]{1,0:T(8,128)}, f32[800,100]{1,0:T(8,128)S(1)}, bf16[128,400]{1,0:T(8,128)(2,1)S(1)}, bf16[512,400]{1,0:T(8,128)(2,1)S(1)}) custom-call(f32[2,208,512]{2,1,0:T(8,128)S(1)} %copy-done.1, bf16[4,128,128]{2,1,0:T(8,128)(2,1)S(1)} %copy-done.2, f32[32,128]{1,0:T(8,128)S(1)} %copy-done.3, bf16[2,16,400,128]{3,2,1,0:T(8,128)(2,1)S(1)} %copy-done), custom_call_target="tpu_custom_call" | custom-call | tf_op jit(solution)/shard_map/pallas_call | solution.py:713
  118.6 0.1 reshape.36
  118.7 1.1 copy.20
  119.9 0.7 copy.21
  120.6 0.9 copy.22
  (3 shorter events, 0.1 us)
Async XLA Ops:
  108.6 1.9 %copy-start = (bf16[2,16,400,128]{3,2,1,0:T(8,128)(2,1)S(1)}, bf16[2,16,400,128]{3,2,1,0:T(8,128)(2,1)}, u32[]{:S(2)}) copy-start(bf16[2,16,400,128]{3,2,1,0:T(8,128)(2,1)} %get-tuple-element.15.v) | copy-start | bytes 9830404
  110.6 1.2 copy-start.1
  111.7 0.9 copy-start.2
  112.6 0.7 copy-start.3

commit v3 on v2

v3 whole, which is shorter than its diff:
```python
import jax
import jax.numpy as jnp
from jax import lax
from jax.experimental import pallas as pl
from jax.experimental.pallas import tpu as pltpu
from jax.sharding import PartitionSpec as P

BLK = 8
FE = 100
HH = 400
UR = 208
PK = 656
HA = 336
PARTS = ((0, HA), (HA, PK - HA))
MESH = pl.DeviceIdType.MESH
F32 = jnp.float32
BF = jnp.bfloat16


def fold_tail(tail):
    tail = jnp.concatenate([tail, jnp.zeros((16, 128), F32)], axis=0)
    out = tail[0:32]
    for g in range(1, 7):
        out = out + pltpu.roll(tail[32 * g : 32 * g + 32], 16 * g, 1)
    return out


def unfold_tail(packed):
    packed = packed.astype(F32)
    rows = [packed] + [pltpu.roll(packed, 128 - 16 * g, 1) for g in range(1, 7)]
    return jnp.concatenate(rows, axis=0)[:UR]


def kernel(
    slots, w_in, w_out, gain, lscale, patches, upstream, gin_out, gout_out, gp_out, vis_out,
    xin, uin, nsc, rsc, RM, VC, PM, WB, wu, GU, U, WT, C2, XU, XP, CT, hacc, S, ST, PG, rb1, rb2, ra1, ra2, fin, GS,
    M, MR, zrm, zrp, V, GP, cen,
    ag_s, ag_r, rs_s, rs_r, vg_s, vg_r, vf_s, vf_r, sq_s, sq_r, zz_s, zz_r, mi_s, mi_r, loc,
):
    dp = lax.axis_index("dp")
    z = lax.axis_index("mp")
    c = lax.rem(dp, 2)
    x = lax.rem(dp // 2, 4)
    y = dp // 8
    me = y * 4 + x
    UU = (0, 1)

    def chip_of(u, da, db):
        if u == 0:
            return lax.rem(y + db, 4) * 4 + lax.rem(x + da, 4)
        return lax.rem(y + da, 4) * 4 + lax.rem(x + db, 4)

    def dev(u, da, db):
        return (chip_of(u, da, db) * 2 + c, z)

    def zdev(dz):
        return (dp, lax.rem(z + dz, 8))

    sib = (me * 2 + 1 - c, z)
    ap = [dev(u, 1, 0) for u in UU]
    am = [dev(u, 3, 0) for u in UU]
    bp = [dev(u, 0, 1) for u in UU]
    bm = [dev(u, 0, 3) for u in UU]
    nbrs = [sib, ap[0], am[0], bp[0], bm[0], zdev(1), zdev(7)]

    def rc(src, dst, ss, rs, d):
        return pltpu.make_async_remote_copy(
            src_ref=src, dst_ref=dst, send_sem=ss, recv_sem=rs, device_id=d, device_id_type=MESH
        )

    def uidx(u, da, db):
        return chip_of(u, da, db) * 2 + (c if u == 0 else 1 - c)

    def da_of(k):
        return k + k // 2 - 2 * (k // 3)

    get_p = pltpu.make_async_copy(patches, xin, loc.at[1])
    get_u = pltpu.make_async_copy(upstream, uin, loc.at[2])
    get_p.start()
    get_u.start()
    barrier = pltpu.get_barrier_semaphore()
    for d in nbrs:
        pl.semaphore_signal(barrier, inc=1, device_id=d, device_id_type=MESH)

    WB[0:FE, 0:800] = w_in[...].astype(F32)
    WB[FE : 2 * FE, 0:800] = w_out[...].astype(F32)
    at = lax.broadcasted_iota(jnp.int32, (8, 800), 1)
    at = jnp.where(at < HH, at, at - HH)
    slot0 = slots[0].astype(F32)
    slot1 = slots[1].astype(F32)
    WB[2 * FE : UR, 0:800] = jnp.where(at == 0, slot0, jnp.where(at == 1, slot1, 0.0))
    for h in (0, 1):
        part = WB[:, 0:512] if h == 0 else pltpu.roll(WB[:, 384:896], 496, 1)
        for t in range(3):
            wu[h, UR * t : UR * t + UR] = part[:, 128 * t : 128 * t + 128].astype(BF)
        tail = part[:, 384:512]
        tail = jnp.where(lax.broadcasted_iota(jnp.int32, tail.shape, 1) < 16, tail, 0.0)
        wu[h, 3 * UR : PK] = fold_tail(tail).astype(BF)
    pl.semaphore_wait(barrier, len(nbrs))

    class Gather:
        def __init__(self, slot, ss, rs):
            self.slot, self.ss, self.rs = slot, ss, rs

        def copy(self, u, m, p, da, db, d):
            ref = self.slot(u, p, da, db)
            return rc(ref, ref, self.ss.at[u, m, p], self.rs.at[u, m, p], d)

        def send(self, u, m, p, da, db, d):
            self.copy(u, m, p, da, db, d).start()

        def wait(self, u, m, p, da, db):
            self.copy(u, m, p, da, db, sib).wait_recv()

        def bsend(self, u, k, p):
            da = da_of(k)
            self.send(u, 3 + 3 * k, p, da, 0, bp[u])
            self.send(u, 4 + 3 * k, p, da, 0, bm[u])

        def start_a(self, u):
            self.send(u, 0, 0, 0, 0, ap[u])
            self.send(u, 1, 1, 0, 0, am[u])
            self.send(u, 0, 1, 0, 0, ap[u])
            self.send(u, 1, 0, 0, 0, am[u])

        def start_b(self, u):
            self.send(u, 3, 0, 0, 0, bp[u])
            self.send(u, 4, 1, 0, 0, bm[u])
            self.send(u, 3, 1, 0, 0, bp[u])
            self.send(u, 4, 0, 0, 0, bm[u])

        def near0(self, u):
            self.wait(u, 0, 0, 3, 0)
            self.send(u, 2, 0, 3, 0, ap[u])
            self.wait(u, 1, 1, 1, 0)
            self.send(u, 2, 1, 1, 0, am[u])
            self.bsend(u, 2, 0)
            self.bsend(u, 1, 1)

        def near1(self, u):
            self.wait(u, 0, 1, 3, 0)
            self.bsend(u, 2, 1)
            self.wait(u, 1, 0, 1, 0)
            self.bsend(u, 1, 0)

        def far(self, u):
            self.wait(u, 2, 0, 2, 0)
            self.bsend(u, 3, 0)
            self.wait(u, 2, 1, 2, 0)
            self.bsend(u, 3, 1)

        def bfwd(self, u, k):
            da = da_of(k)
            self.wait(u, 3 + 3 * k, 0, da, 3)
            self.send(u, 5 + 3 * k, 0, da, 3, bp[u])
            self.wait(u, 4 + 3 * k, 1, da, 1)
            self.send(u, 5 + 3 * k, 1, da, 1, bm[u])

        def brest(self, u, k):
            da = da_of(k)
            self.wait(u, 3 + 3 * k, 1, da, 3)
            self.wait(u, 4 + 3 * k, 0, da, 1)

        def blast(self, u, k):
            da = da_of(k)
            self.wait(u, 5 + 3 * k, 0, da, 2)
            self.wait(u, 5 + 3 * k, 1, da, 2)

        def done(self):
            def body(m, carry):
                for u in UU:
                    for p in (0, 1):
                        self.copy(u, m, p, 0, 0, sib).wait_send()
                return carry

            lax.fori_loop(0, 15, body, 0)

    def wslot(u, p, da, db):
        return U.at[uidx(u, da, db), pl.ds(*PARTS[p])]

    ag = Gather(wslot, ag_s, ag_r)

    to_sib = rc(wu.at[1 - c], U.at[me * 2 + c], mi_s.at[0], mi_r.at[0], sib)
    to_sib.start()
    own = pltpu.make_async_copy(wu.at[c], U.at[me * 2 + c], loc.at[0])
    own.start()
    own.wait()
    ag.start_a(0)
    ag.start_b(0)
    rc(wu.at[0], U.at[me * 2 + 1 - c], mi_s.at[0], mi_r.at[0], sib).wait_recv()
    ag.start_a(1)
    ag.start_b(1)

    hacc[...] = jnp.zeros_like(hacc)
    get_p.wait()
    get_u.wait()

    def act_step(r, carry):
        r0 = pl.multiple_of(r * 16, 16)
        xs = xin[pl.ds(r0, 16), :].astype(F32)
        root = jnp.sqrt(jnp.sum(xs * xs, axis=1, keepdims=True) * (1.0 / 3200.0) + 1e-06)
        RM[pl.ds(r0, 16), :] = jnp.broadcast_to(root, (16, 128))
        up_live = uin[pl.ds(r0, 16), :].astype(F32)
        up_live = up_live * jnp.where(slots[r // 4] >= 0, 1.0, 0.0)
        nsc[0] = xs / root * VC[0, 0:1, :]
        nsc[1] = up_live * VC[1, 0:1, :]
        rsc[0] = up_live
        rsc[1] = xs
        lane = lax.broadcasted_iota(jnp.int32, (16, 256), 1)
        for i in range(32):
            q = min(100 * i // 128, 23)
            sh = 100 * i - 128 * q
            win = slice(128 * q, 128 * q + 256)
            a = pltpu.roll(nsc[0, :, win], (256 - sh) % 256, 1)
            b = pltpu.roll(nsc[1, :, win], (100 - sh) % 256, 1)
            both = jnp.where(lane < FE, a, jnp.where(lane < 2 * FE, b, 0.0))
            C2[c, i, pl.ds(r0, 16), :] = both.astype(BF)
            a = pltpu.roll(rsc[0, :, win], (256 - sh) % 256, 1)
            b = pltpu.roll(rsc[1, :, win], (4 - sh) % 256, 1)
            XU[i, pl.ds(r0, 16), :] = a[:, :128].astype(BF)
            XP[i, pl.ds(r0, 16), :] = b[:, :128].astype(BF)
        return carry

    for q in range(25):
        VC[0, :, 128 * q : 128 * q + 128] = jnp.broadcast_to(gain[q : q + 1, :], (8, 128))
        VC[1, :, 128 * q : 128 * q + 128] = jnp.broadcast_to(lscale[q : q + 1, :], (8, 128))
    for i in range(32):
        q = min(100 * i // 128, 23)
        sh = 100 * i - 128 * q
        win = slice(128 * q, 128 * q + 256)
        GU[0, i] = pltpu.roll(VC[0, :, win], (256 - sh) % 256, 1)[:, :128]
        GU[1, i] = pltpu.roll(VC[1, :, win], (4 - sh) % 256, 1)[:, :128]
    lax.fori_loop(0, 8, act_step, 0)
    act_sib = rc(C2.at[c], C2.at[c], mi_s.at[1], mi_r.at[1], sib)
    act_sib.start()
    to = lax.broadcasted_iota(jnp.int32, (512, 256), 0)
    fr = lax.rem(lax.broadcasted_iota(jnp.int32, (512, 256), 1), 64)
    same = fr == 32 * (to // 256) + 2 * lax.rem(to, 16) + lax.rem(to // 128, 2)
    PM[...] = jnp.where(same, (dp * BLK + lax.rem(to // 16, 8)).astype(F32), -5.0)

    def weight(i):
        w = U[i]
        return jnp.concatenate([w[0:208], w[208:416], w[416:624], WT[i]], axis=1)

    def up(i):
        act = jnp.concatenate([C2[0, i], C2[1, i]], axis=0)
        CT[i] = act.T[:UR]
        a = act[:, :UR]
        first = lax.broadcasted_iota(jnp.int32, a.shape, 1) < FE
        zero = jnp.zeros_like(a)
        lhs = jnp.concatenate([jnp.where(first, a, zero), jnp.where(first, zero, a)], axis=0)
        WT[i] = unfold_tail(U[i, 3 * UR : PK]).astype(BF)
        hacc[...] += jnp.dot(lhs, weight(i), preferred_element_type=F32)

    def up_all(units):
        for u, da, db in units:
            up(uidx(u, da, db))

    for u in UU:
        ag.near0(u)
    for u in UU:
        ag.near1(u)
    rc(C2.at[c], C2.at[1 - c], mi_s.at[1], mi_r.at[1], sib).wait_recv()
    for u in UU:
        ag.bfwd(u, 0)
    up_all([(0, 0, 0), (1, 0, 0)])
    for u in UU:
        ag.far(u)
    up_all([(u, da, 0) for u in UU for da in (3, 1)])

    def fwd_step(k, carry):
        for u in UU:
            ag.bfwd(u, k)
        for u in UU:
            ag.brest(u, k - 1)
        up_all([(u, da_of(k - 1), db) for u in UU for db in (3, 1)])
        return carry

    lax.fori_loop(1, 4, fwd_step, 0)
    up_all([(0, 2, 0), (1, 2, 0)])

    def last_step(k, carry):
        for u in UU:
            ag.blast(u, k)
        up_all([(u, da_of(k), 2) for u in UU])
        return carry

    lax.fori_loop(0, 3, last_step, 0)
    for u in UU:
        ag.brest(u, 3)
    up_all([(u, da_of(3), db) for u in UU for db in (3, 1)])
    last_step(3, 0)

    def gelu_step(r, carry):
        r0 = pl.multiple_of(r * 32, 32)
        h = hacc[pl.ds(r0, 32), :]
        gh = hacc[pl.ds(r0 + 256, 32), :]
        valid = lax.broadcasted_iota(jnp.int32, h.shape, 1) < HH
        cumul = 0.5 * (1.0 + lax.erf(h * 0.7071067811865476))
        density = jnp.exp(-0.5 * h * h) * 0.3989422804014327
        ho = jnp.where(valid, h * cumul, 0.0).astype(BF)
        gi = jnp.where(valid, gh * (cumul + h * density), 0.0).astype(BF)
        S[pl.ds(r0, 32), :] = gi
        S[pl.ds(r0 + 256, 32), :] = ho
        row = jnp.sum(gi.astype(F32) * jnp.where(valid, h, 0.0), axis=1, keepdims=True)
        cen[pl.ds(r0, 32), :] = jnp.broadcast_to(row, (32, 128))
        return carry

    lax.fori_loop(0, 8, gelu_step, 0)

    def down(i):
        ct = CT[i]
        first = lax.broadcasted_iota(jnp.int32, ct.shape, 0) < FE
        zero = jnp.zeros_like(ct)
        lhs = jnp.concatenate([jnp.where(first, ct, zero), jnp.where(first, zero, ct)], axis=1)
        out = jnp.dot(lhs, S[...], preferred_element_type=F32)
        return [out[:, 0:128], out[:, 128:256], out[:, 256:384], fold_tail(out[:, 384:512])]

    ROWS4 = ((0, 208), (208, 416), (416, 624), (624, 656))

    def store_unit(i, *adds):
        for (lo, hi), part in zip(ROWS4, down(i)):
            for ref in adds:
                part = part + ref[lo:hi].astype(F32)
            PG[i, lo:hi] = part.astype(BF)

    def add_part(i, p, ref):
        lo, n = PARTS[p]
        PG[i, lo : lo + n] = (PG[i, lo : lo + n].astype(F32) + ref[lo : lo + n].astype(F32)).astype(BF)

    def rs(u, m, p, i, buf, d):
        return rc(
            PG.at[i, pl.ds(*PARTS[p])], buf.at[pl.ds(*PARTS[p])], rs_s.at[u, m, p], rs_r.at[u, m, p], d
        )

    def rs_wait(u, m, p, buf):
        rs(u, m, p, 0, buf, sib).wait_recv()

    def first_down(kk, carry):
        k = 3 - kk
        for u in UU:
            i = uidx(u, da_of(k), 2)
            store_unit(i)
            rs(u, 3 + 3 * k, 0, i, rb1.at[u, k], bp[u]).start()
            rs(u, 3 + 3 * k, 1, i, rb1.at[u, k], bm[u]).start()
        return carry

    def second_free(k):
        for u in UU:
            i = uidx(u, da_of(k), 1)
            store_unit(i)
            rs(u, 4 + 3 * k, 1, i, rb2.at[u, 0, k], bp[u]).start()
            i = uidx(u, da_of(k), 3)
            store_unit(i)
            rs(u, 5 + 3 * k, 0, i, rb2.at[u, 1, k], bm[u]).start()

    def second_sum(k):
        for u in UU:
            i = uidx(u, da_of(k), 1)
            rs_wait(u, 3 + 3 * k, 0, rb1.at[u, k])
            add_part(i, 0, rb1.at[u, k])
            rs(u, 4 + 3 * k, 0, i, rb2.at[u, 0, k], bp[u]).start()
            i = uidx(u, da_of(k), 3)
            rs_wait(u, 3 + 3 * k, 1, rb1.at[u, k])
            add_part(i, 1, rb1.at[u, k])
            rs(u, 5 + 3 * k, 1, i, rb2.at[u, 1, k], bm[u]).start()

    def second_down(kk, carry):
        second_free(3 - kk)
        second_sum(3 - kk)
        return carry

    def third(u, k):
        for w in (0, 1):
            for p in (1, 0) if w == 0 else (0, 1):
                rs_wait(u, 4 + 3 * k + w, p, rb2.at[u, w, k])
        i = uidx(u, da_of(k), 0)
        store_unit(i, rb2.at[u, 0, k], rb2.at[u, 1, k])
        return i

    def zblk(r):
        return lax.rem(z + r, 8)

    def mix(b):
        def body(j, carry):
            i = b * 4 + j
            w = weight(i)
            m = jnp.dot(w[96:208], ST[:, 256:512], preferred_element_type=F32)
            row = lax.broadcasted_iota(jnp.int32, m.shape, 0)
            m = jnp.where(row == 104, cen_hi, jnp.where(row == 105, cen_lo, m)).astype(BF)
            n = jnp.dot(w[0:112], ST[:, 0:256], preferred_element_type=F32).astype(BF)
            for e in (0, 1):
                M[e, 0, i] = m[:, 128 * e : 128 * e + 128]
                M[e, 1, i] = n[:, 128 * e : 128 * e + 128]
            return carry

        lax.fori_loop(0, 4, body, 0)

    def to_sibling(s, r):
        b = 4 * zblk(r)
        return rc(
            M.at[1 - c, :, pl.ds(b, 4)], MR.at[:, pl.ds(b, 4)], sq_s.at[s], sq_r.at[s], sib
        )

    zorder = (4, 3, 5, 2, 6, 1, 7, 0)

    def mix_step(s, carry):
        h = (s + 1) // 2
        r = 4 + h - 2 * h * lax.rem(s, 2)
        mix(zblk(r))
        to_sibling(s, r).start()
        return carry

    def zcopy(t, way, j, h):
        r = 4 + j if way == 0 else 4 - j
        buf = zrm if way == 0 else zrp
        return rc(
            M.at[c, t, pl.ds(4 * zblk(r) + 2 * h, 2)], buf.at[t, j, pl.ds(2 * h, 2)],
            zz_s.at[t, way, j, h], zz_r.at[t, way, j, h], zdev(7 if way == 0 else 1),
        )

    def combine(t, r, h, ref):
        b = zblk(r)
        for j in (2 * h, 2 * h + 1):
            i = b * 4 + j
            v = M[c, t, i].astype(F32) + MR[t, i].astype(F32)
            if ref is not None:
                v = v + ref[j].astype(F32)
            M[c, t, i] = v.astype(BF)

    def zfirst(t):
        if t == 0:
            to_sibling(0, 4).wait_recv()
        for way in (0, 1):
            combine(t, 4, way, None)
            zcopy(t, way, 0, way).start()

    def zstep(t, j):
        for n in (0, 1):
            for way in (0, 1):
                buf = zrm if way == 0 else zrp
                r = 4 + j if way == 0 else 4 - j
                if n == 0 and t == 0:
                    to_sibling(2 * j if way == 0 else 2 * j - 1, r).wait_recv()
                h = (1 - way if n == 0 else way) if j == 1 else n
                if j == 1 and n == 0:
                    combine(t, r, h, None)
                else:
                    zcopy(t, way, j - 1, h).wait_recv()
                    combine(t, r, h, buf.at[t, j - 1])
                zcopy(t, way, j, h).start()

    def zlast(t, j):
        i = z * 4 + j
        v = M[c, t, i].astype(F32) + MR[t, i].astype(F32)
        v = v + zrm[t, 3, j].astype(F32) + zrp[t, 3, j].astype(F32)
        return jnp.concatenate([v, jnp.zeros((16, 128), F32)], axis=0).T

    lax.fori_loop(0, 2, first_down, 0)
    ST[...] = S[...].T
    center = cen[...].T[0:1]
    cen_hi = center.astype(BF).astype(F32)
    cen_lo = center - cen_hi
    lax.fori_loop(0, 2, mix_step, 0)
    lax.fori_loop(2, 4, first_down, 0)
    lax.fori_loop(2, 4, mix_step, 0)
    zfirst(0)
    second_free(3)
    lax.fori_loop(4, 8, mix_step, 0)
    zstep(0, 1)
    zfirst(1)
    second_sum(3)
    lax.fori_loop(1, 4, second_down, 0)
    zstep(0, 2)
    zstep(1, 1)

    for u in UU:
        i = third(u, 3)
        rs(u, 0, 0, i, ra1.at[u], ap[u]).start()
        rs(u, 0, 1, i, ra1.at[u], am[u]).start()
    for u in UU:
        i = third(u, 2)
        rs(u, 2, 0, i, ra2.at[u, 1], am[u]).start()
    zstep(0, 3)
    zstep(1, 2)
    for u in UU:
        i = third(u, 1)
        rs(u, 1, 1, i, ra2.at[u, 0], ap[u]).start()
    for u in UU:
        rs_wait(u, 0, 0, ra1.at[u])
        i = uidx(u, 1, 0)
        add_part(i, 0, ra1.at[u])
        rs(u, 1, 0, i, ra2.at[u, 0], ap[u]).start()
        rs_wait(u, 0, 1, ra1.at[u])
        i = uidx(u, 3, 0)
        add_part(i, 1, ra1.at[u])
        rs(u, 2, 1, i, ra2.at[u, 1], am[u]).start()

    to_sibling(7, 0).wait_recv()
    for h in (0, 1):
        for way in (0, 1):
            zcopy(0, way, 3, h).wait_recv()
    ln = lax.broadcasted_iota(jnp.int32, (128, 128), 1)
    wide = [jnp.zeros((128, 128), F32) for _ in range(4)]
    centre = None
    for j in range(4):
        t = zlast(0, j)
        if j == 0:
            centre = (t[:, 104:105] + t[:, 105:106]) * (1.0 / 3200.0)
        i = z * 4 + j
        r = XP[i].astype(F32) + GU[1, i][0:1] * t
        at, sh = divmod(FE * j, 128)
        r = pltpu.roll(r, (sh + 124) % 128, 1)
        wide[at] = jnp.where((ln >= sh) & (ln < sh + FE), r, wide[at])
        if sh + FE > 128:
            wide[at + 1] = jnp.where(ln < sh + FE - 128, r, wide[at + 1])
    cen[0:128, :] = jnp.broadcast_to(centre, (128, 128))
    tail = jnp.where(ln < 16, wide[3], 0.0)
    folded = tail[0:16]
    for g in range(1, 8):
        folded = folded + pltpu.roll(tail[16 * g : 16 * g + 16], 16 * g, 1)
    for t in range(3):
        V[c, me, 128 * t : 128 * t + 128, :] = wide[t].astype(BF)
    V[c, me, 384:400, :] = folded.astype(BF)

    VP = (((0, 112), (112, 96)), ((208, 96), (304, 96)))

    def vslot(u, p, da, db):
        return V.at[c, chip_of(u, da, db), pl.ds(*VP[u][p])]

    vg = Gather(vslot, vg_s, vg_r)

    def fwd(u, da, db):
        ch = chip_of(u, da, db)
        ref = V.at[c, ch, pl.ds(208 * u, 208 - 16 * u)]
        return rc(ref, ref, vf_s.at[u, ch], vf_r.at[u, ch], sib)

    for u in UU:
        vg.start_a(u)
    for u in UU:
        vg.start_b(u)
    for u in UU:
        fwd(u, 0, 0).start()

    def finish(u):
        for w in (0, 1):
            for p in (1, 0) if w == 0 else (0, 1):
                rs_wait(u, 4 + w, p, rb2.at[u, w, 0])
        i = uidx(u, 0, 0)
        parts = down(i)
        for w in (0, 1):
            for p in (1, 0) if w == 0 else (0, 1):
                rs_wait(u, 1 + w, p, ra2.at[u, w])
        out = []
        for (lo, hi), part in zip(ROWS4, parts):
            for ref in (rb2.at[u, 0, 0], rb2.at[u, 1, 0], ra2.at[u, 0], ra2.at[u, 1]):
                part = part + ref[lo:hi].astype(F32)
            out.append(part)
        return i, out

    zstep(1, 3)
    i, parts = finish(1)
    for (lo, hi), part in zip(ROWS4, parts):
        PG[i, lo:hi] = part.astype(BF)
    to_fin = rc(PG.at[i], fin, mi_s.at[2], mi_r.at[2], sib)
    to_fin.start()
    for u in UU:
        vg.near0(u)
    for u in UU:
        vg.near1(u)
    for u in UU:
        fwd(u, 3, 0).start()
        fwd(u, 1, 0).start()
    for u in UU:
        vg.bfwd(u, 0)
    _, parts = finish(0)
    for t in range(3):
        GS[:, 128 * t : 128 * t + 128] = parts[t]
    GS[:, 384:512] = unfold_tail(parts[3])
    for u in UU:
        vg.far(u)
        fwd(u, 2, 0).start()

    hacc[...] = jnp.zeros_like(hacc)

    for h in (0, 1):
        for way in (0, 1):
            zcopy(1, way, 3, h).wait_recv()
    root = RM[:, 0:1]
    centre = cen[0:128, 0:1]
    for j in range(4):
        i = z * 4 + j
        t = zlast(1, j)
        moved = pltpu.roll(XP[i].astype(F32), 124, 1)
        gp = XU[i].astype(F32) + (GU[0, i][0:1] * t - moved / root * centre) / root
        GP[FE * j : FE * j + FE, :] = gp.T[:FE]
    gp_out[...] = GP[...].astype(BF)

    def take(ch):
        for u in UU:
            ref = V.at[1 - c, ch, pl.ds(208 * u, 208 - 16 * u)]
            rc(ref, ref, vf_s.at[u, ch], vf_r.at[u, ch], sib).wait_recv()
        rows = []
        blocks = []
        ln = lax.broadcasted_iota(jnp.int32, (1, 128), 1)
        for e in (0, 1):
            tail = V[e, ch, 384:400].astype(F32)
            tail = [tail] + [pltpu.roll(tail, 128 - 16 * g, 1) for g in range(1, 8)]
            tail = jnp.concatenate(tail, axis=0).astype(BF)
            rows.append(
                jnp.concatenate([V[e, ch, 128 * t : 128 * t + 128] for t in range(3)] + [tail], axis=1)
            )
            pair = U[2 * ch + e, 192:208].astype(F32)[8:9]
            blocks.append(jnp.where(ln < 64, pair[:, 0:1], pair[:, 1:2]))
        place = (PM[...] == jnp.concatenate(blocks, axis=1)).astype(BF)
        hacc[...] += jnp.dot(place, jnp.concatenate(rows, axis=0), preferred_element_type=F32)

    def take4(kind):
        def body(n, carry):
            h, m = n // 2, lax.rem(n, 2)
            if kind == 0:
                dx, dy = (1 - m) * (n + 1), m * n
            elif kind == 1:
                dx, dy = 1 + 2 * m, 1 + 2 * h
            else:
                dx, dy = 2 * (1 - h) + h * (1 + 2 * m), (1 - h) * (1 + 2 * m) + 2 * h
            take(lax.rem(y + dy, 4) * 4 + lax.rem(x + dx, 4))
            return carry

        lax.fori_loop(0, 4, body, 0)

    def vstep(k, carry):
        for u in UU:
            vg.bfwd(u, k)
        for u in UU:
            vg.brest(u, k - 1)
            fwd(u, da_of(k - 1), 3).start()
            fwd(u, da_of(k - 1), 1).start()
        return carry

    take(me)
    vstep(1, 0)
    take4(0)
    lax.fori_loop(2, 4, vstep, 0)

    to_fin.wait_recv()
    mine = GS[...]
    other = [fin[208 * t : 208 * t + 208].astype(F32) for t in range(3)] + [unfold_tail(fin[624:656])]
    other = jnp.concatenate(other, axis=1)
    for h in (0, 1):
        half = jnp.where(c == h, mine, other)
        gin_out[:, HH * h : HH * h + HH] = half[0:FE, 0:HH]
        gout_out[:, HH * h : HH * h + HH] = half[FE : 2 * FE, 0:HH]

    take4(1)
    for u in UU:
        vg.brest(u, 3)
        fwd(u, 2, 3).start()
        fwd(u, 2, 1).start()
    for k in range(4):
        for u in UU:
            vg.blast(u, k)
            fwd(u, da_of(k), 2).start()
        if k == 0:
            take(lax.rem(y, 4) * 4 + lax.rem(x + 2, 4))
            take(lax.rem(y + 2, 4) * 4 + x)
        if k == 2:
            take4(2)
    take(lax.rem(y + 2, 4) * 4 + lax.rem(x + 2, 4))
    for q in range(4):
        vis_out[q] = hacc[128 * q : 128 * q + 128, :].astype(BF).T[:HH]

    def vfwd_wait(ch, carry):
        for u in UU:
            ref = V.at[1 - c, ch, pl.ds(208 * u, 208 - 16 * u)]
            rc(ref, ref, vf_s.at[u, ch], vf_r.at[u, ch], sib).wait_send()
        return carry

    lax.fori_loop(0, 16, vfwd_wait, 0)

    ag.done()
    vg.done()
    to_sib.wait_send()
    act_sib.wait_send()
    to_fin.wait_send()
    for s in range(8):
        to_sibling(s, zorder[s]).wait_send()
    for t in (0, 1):
        for way in (0, 1):
            zcopy(t, way, 0, way).wait_send()
            for j in (1, 2, 3):
                for h in (0, 1):
                    zcopy(t, way, j, h).wait_send()

    def rs_done(m, carry):
        for u in UU:
            for p in (0, 1):
                rs(u, m, p, 0, ra1.at[u], sib).wait_send()
        return carry

    lax.fori_loop(0, 15, rs_done, 0)


def mega(slots, w_in, w_out, gain, lscale, patches, upstream):
    dma = pltpu.SemaphoreType.DMA
    vm = pl.BlockSpec(memory_space=pltpu.VMEM)
    sm = pl.BlockSpec(memory_space=pltpu.SMEM)
    hbm = pl.BlockSpec(memory_space=pl.ANY)
    return pl.pallas_call(
        kernel,
        out_shape=(
            jax.ShapeDtypeStruct((FE, 2 * HH), F32),
            jax.ShapeDtypeStruct((FE, 2 * HH), F32),
            jax.ShapeDtypeStruct((HH, 128), BF),
            jax.ShapeDtypeStruct((4, HH, BLK * 16), BF),
        ),
        in_specs=[sm, vm, vm, vm, vm, hbm, hbm],
        out_specs=(vm, vm, vm, vm),
        scratch_shapes=[
            pltpu.VMEM((128, 3200), BF),
            pltpu.VMEM((128, 3200), BF),
            pltpu.VMEM((2, 16, 3200), F32),
            pltpu.VMEM((2, 16, 3200), F32),
            pltpu.VMEM((128, 128), F32),
            pltpu.VMEM((2, 8, 3200), F32),
            pltpu.VMEM((512, 256), F32),
            pltpu.VMEM((UR, 896), F32),
            pltpu.VMEM((2, PK, 128), BF),
            pltpu.VMEM((2, 32, 8, 128), F32),
            pltpu.VMEM((32, PK, 128), BF),
            pltpu.VMEM((32, UR, 128), BF),
            pltpu.VMEM((2, 32, 128, 256), BF),
            pltpu.VMEM((32, 128, 128), BF),
            pltpu.VMEM((32, 128, 128), BF),
            pltpu.VMEM((32, UR, 256), BF),
            pltpu.VMEM((512, 512), F32),
            pltpu.VMEM((512, 512), BF),
            pltpu.VMEM((512, 512), BF),
            pltpu.VMEM((32, PK, 128), BF),
            pltpu.VMEM((2, 4, PK, 128), BF),
            pltpu.VMEM((2, 2, 4, PK, 128), BF),
            pltpu.VMEM((2, PK, 128), BF),
            pltpu.VMEM((2, 2, PK, 128), BF),
            pltpu.VMEM((PK, 128), BF),
            pltpu.VMEM((UR, 512), F32),
            pltpu.VMEM((2, 2, 32, 112, 128), BF),
            pltpu.VMEM((2, 32, 112, 128), BF),
            pltpu.VMEM((2, 4, 4, 112, 128), BF),
            pltpu.VMEM((2, 4, 4, 112, 128), BF),
            pltpu.VMEM((2, 16, 400, 128), BF),
            pltpu.VMEM((HH, 128), F32),
            pltpu.VMEM((256, 128), F32),
            dma((2, 15, 2)), dma((2, 15, 2)),
            dma((2, 15, 2)), dma((2, 15, 2)),
            dma((2, 15, 2)), dma((2, 15, 2)),
            dma((2, 16)), dma((2, 16)),
            dma((8,)), dma((8,)),
            dma((2, 2, 4, 2)), dma((2, 2, 4, 2)),
            dma((3,)), dma((3,)),
            dma((3,)),
        ],
        compiler_params=pltpu.CompilerParams(
            collective_id=0, has_side_effects=True, vmem_limit_bytes=60 * 2**20
        ),
    )(slots, w_in, w_out, gain, lscale, patches, upstream)


def shards(patches, upstream, norm_gain, layer_scale, w_in, w_out, slot_block):
    grad_w_in, grad_w_out, grad_patches, vision = mega(
        slot_block, w_in, w_out.T, norm_gain.reshape(25, 128), layer_scale.reshape(25, 128), patches, upstream
    )
    return (vision.transpose(2, 0, 1), grad_patches.T, grad_w_in, grad_w_out.T)


def solution(mesh):
    return jax.shard_map(
        shards,
        mesh=mesh,
        in_specs=(P("dp", None), P("dp", None), P(), P(), P("dp", "mp"), P("mp", "dp"), P("dp")),
        out_specs=(P("dp", None, "mp"), P("dp", "mp"), P("dp", "mp"), P("mp", "dp")),
        check_vma=False,
    )
```

time: 122 us -> 105 us (0.86)
  local copies, waits for them, and re-layouts: 12.2 us -> 4.35 us
  Pallas kernels: 104 us -> 99.6 us
  other arithmetic: 4.27 us -> 0 us
    pallas_call x2 -> x1, Pallas kernels: 104 us -> 99.6 us  [mega(): pl.pallas_call(kernel, out_shape=(jax.ShapeDtypeStruct((FE, 2 * HH), F32)...]
    unnamed x11 -> x10, local copies, waits for them, and re-layouts: 7.53 us -> 4.35 us
    broadcast_in_dim x5 -> x0, local copies, waits for them, and re-layouts: 2.33 us -> none  [the longest x2 1.46 us: shards(): vec = jnp.concatenate([norm_gain[None], layer_scale[None], units], axis=0)]
    reshape x7 -> x0, local copies, waits for them, and re-layouts: 2.1 us -> none  [the longest x1 0.82 us: shards(): norm_gain.reshape(32, FE)]
    concatenate x3 -> x0, other arithmetic: 2.05 us -> none  [the longest x1 1.08 us: pack_units(): both = jnp.concatenate([w_in, w_out.T, table], axis=0)]
where the time goes in v3:
time: 105 us
  Pallas kernels  99.6 us (95%)
  local copies, waits for them, and re-layouts  4.35 us (4%)
    pallas_call x1, Pallas kernels, mega(): pl.pallas_call(kernel, out_shape=(jax.ShapeDtypeStruct((FE, 2 * HH), F32)...  99.6 us
    unnamed x10, local copies, waits for them, and re-layouts  4.35 us

profile of v3, /device:TPU:1, one launch (start us, length us, event | category | flops | bytes accessed | tf_op | source)
XLA Modules:
  0.0 104.7 jit_solution(18266182817174486326)
XLA Ops:
  0.6 99.6 %shard_map.102 = (f32[100,800]{1,0:T(8,128)}, f32[100,800]{1,0:T(8,128)}, bf16[400,128]{1,0:T(8,128)(2,1)}, bf16[4,400,128]{2,1,0:T(8,128)(2,1)}) custom-call(s32[2]{0:T(128)} %slots.1, bf16[100,800]{1,0:T(8,128)(2,1)} %w_in.1, bf16[100,800]{1,0:T(8,128)(2,1)} %bitcast.8, f32[25,128]{1,0:T(8,128)} %bitcast.10, f32[25,128]{1,0:T(8,128)} %bitcast.11, ...), custom_call_target="tpu_custom_call" | custom-call | tf_op jit(solution)/shard_map/pallas_call | solution.py:709
  100.3 0.0 copy-start.2
  100.3 0.0 copy-start.1
  100.3 1.8 %copy.15 = bf16[128,4,400]{0,2,1:T(8,128)(2,1)} copy(bf16[128,4,400]{0,2,1:T(8,128)(2,1)} %bitcast.6) | data formatting | bytes 819200
  102.1 0.0 copy-done.2
  102.1 0.6 copy.16
  102.8 0.0 copy-done.1
  102.8 0.0 copy-start
  102.8 0.7 copy.17
  103.5 0.4 copy-done
  103.9 0.7 copy.18
Async XLA Ops:
  100.3 1.9 %copy-start.2 = (bf16[400,128]{1,0:T(8,128)(2,1)S(1)}, bf16[400,128]{1,0:T(8,128)(2,1)}, u32[]{:S(2)}) copy-start(bf16[400,128]{1,0:T(8,128)(2,1)} %get-tuple-element.9) | copy-start | bytes 307204
  100.3 2.5 %copy-start.1 = (f32[100,800]{1,0:T(8,128)S(1)}, f32[100,800]{1,0:T(8,128)}, u32[]{:S(2)}) copy-start(f32[100,800]{1,0:T(8,128)} %get-tuple-element.18) | copy-start | bytes 960004
  102.8 1.1 %copy-start = (f32[100,800]{1,0:T(8,128)S(1)}, f32[100,800]{1,0:T(8,128)}, u32[]{:S(2)}) copy-start(f32[100,800]{1,0:T(8,128)} %get-tuple-element.11) | copy-start | bytes 960004

commit v4 on v3

--- a/solution.py
+++ b/solution.py
@@ -33,7 +33,7 @@
 
 def kernel(
     slots, w_in, w_out, gain, lscale, patches, upstream, gin_out, gout_out, gp_out, vis_out,
-    xin, uin, nsc, rsc, RM, VC, PM, WB, wu, GU, U, WT, C2, XU, XP, CT, hacc, S, ST, PG, rb1, rb2, ra1, ra2, fin, GS,
+    xin, uin, nsc, rsc, RM, VC, PM, VT, WB, wu, GU, U, WT, C2, XU, XP, CT, hacc, S, ST, PG, rb1, rb2, ra1, ra2, fin, GS,
     M, MR, zrm, zrp, V, GP, cen,
     ag_s, ag_r, rs_s, rs_r, vg_s, vg_r, vf_s, vf_r, sq_s, sq_r, zz_s, zz_r, mi_s, mi_r, loc,
 ):
@@ -102,12 +102,13 @@
         def __init__(self, slot, ss, rs):
             self.slot, self.ss, self.rs = slot, ss, rs
 
-        def copy(self, u, m, p, da, db, d):
+        def copy(self, u, m, p, da, db, d, src=None):
             ref = self.slot(u, p, da, db)
-            return rc(ref, ref, self.ss.at[u, m, p], self.rs.at[u, m, p], d)
-
-        def send(self, u, m, p, da, db, d):
-            self.copy(u, m, p, da, db, d).start()
+            src = ref if src is None else src.at[c, pl.ds(*PARTS[p])]
+            return rc(src, ref, self.ss.at[u, m, p], self.rs.at[u, m, p], d)
+
+        def send(self, u, m, p, da, db, d, src=None):
+            self.copy(u, m, p, da, db, d, src).start()
 
         def wait(self, u, m, p, da, db):
             self.copy(u, m, p, da, db, sib).wait_recv()
@@ -117,17 +118,17 @@
             self.send(u, 3 + 3 * k, p, da, 0, bp[u])
             self.send(u, 4 + 3 * k, p, da, 0, bm[u])
 
-        def start_a(self, u):
-            self.send(u, 0, 0, 0, 0, ap[u])
-            self.send(u, 1, 1, 0, 0, am[u])
-            self.send(u, 0, 1, 0, 0, ap[u])
-            self.send(u, 1, 0, 0, 0, am[u])
-
-        def start_b(self, u):
-            self.send(u, 3, 0, 0, 0, bp[u])
-            self.send(u, 4, 1, 0, 0, bm[u])
-            self.send(u, 3, 1, 0, 0, bp[u])
-            self.send(u, 4, 0, 0, 0, bm[u])
+        def start_a(self, u, src=None):
+            self.send(u, 0, 0, 0, 0, ap[u], src)
+            self.send(u, 1, 1, 0, 0, am[u], src)
+            self.send(u, 0, 1, 0, 0, ap[u], src)
+            self.send(u, 1, 0, 0, 0, am[u], src)
+
+        def start_b(self, u, src=None):
+            self.send(u, 3, 0, 0, 0, bp[u], src)
+            self.send(u, 4, 1, 0, 0, bm[u], src)
+            self.send(u, 3, 1, 0, 0, bp[u], src)
+            self.send(u, 4, 0, 0, 0, bm[u], src)
 
         def near0(self, u):
             self.wait(u, 0, 0, 3, 0)
@@ -184,9 +185,8 @@
     to_sib.start()
     own = pltpu.make_async_copy(wu.at[c], U.at[me * 2 + c], loc.at[0])
     own.start()
-    own.wait()
-    ag.start_a(0)
-    ag.start_b(0)
+    ag.start_a(0, wu)
+    ag.start_b(0, wu)
     rc(wu.at[0], U.at[me * 2 + 1 - c], mi_s.at[0], mi_r.at[0], sib).wait_recv()
     ag.start_a(1)
     ag.start_b(1)
@@ -233,11 +233,6 @@
     lax.fori_loop(0, 8, act_step, 0)
     act_sib = rc(C2.at[c], C2.at[c], mi_s.at[1], mi_r.at[1], sib)
     act_sib.start()
-    to = lax.broadcasted_iota(jnp.int32, (512, 256), 0)
-    fr = lax.rem(lax.broadcasted_iota(jnp.int32, (512, 256), 1), 64)
-    same = fr == 32 * (to // 256) + 2 * lax.rem(to, 16) + lax.rem(to // 128, 2)
-    PM[...] = jnp.where(same, (dp * BLK + lax.rem(to // 16, 8)).astype(F32), -5.0)
-
     def weight(i):
         w = U[i]
         return jnp.concatenate([w[0:208], w[208:416], w[416:624], WT[i]], axis=1)
@@ -263,6 +258,7 @@
     rc(C2.at[c], C2.at[1 - c], mi_s.at[1], mi_r.at[1], sib).wait_recv()
     for u in UU:
         ag.bfwd(u, 0)
+    own.wait()
     up_all([(0, 0, 0), (1, 0, 0)])
     for u in UU:
         ag.far(u)
@@ -308,15 +304,30 @@
 
     lax.fori_loop(0, 8, gelu_step, 0)
 
+    def down_all(units):
+        lows = jnp.concatenate([CT[i, 0:112] for i in units], axis=0)
+        highs = jnp.concatenate([CT[i, 96:208] for i in units], axis=0)
+        lows = jnp.dot(lows, S[0:256], preferred_element_type=F32)
+        highs = jnp.dot(highs, S[256:512], preferred_element_type=F32)
+        row = lax.broadcasted_iota(jnp.int32, (16, 512), 0)
+        res = []
+        for n in range(len(units)):
+            low, high = lows[112 * n : 112 * n + 112], highs[112 * n : 112 * n + 112]
+            mid = jnp.where(row < 4, low[96:112], high[0:16])
+            out = jnp.concatenate([low[0:96], mid, high[16:112]], axis=0)
+            tail = fold_tail(out[:, 384:512])
+            res.append([out[:, 0:128], out[:, 128:256], out[:, 256:384], tail])
+        return res
+
     def down(i):
-        ct = CT[i]
-        first = lax.broadcasted_iota(jnp.int32, ct.shape, 0) < FE
-        zero = jnp.zeros_like(ct)
-        lhs = jnp.concatenate([jnp.where(first, ct, zero), jnp.where(first, zero, ct)], axis=1)
-        out = jnp.dot(lhs, S[...], preferred_element_type=F32)
-        return [out[:, 0:128], out[:, 128:256], out[:, 256:384], fold_tail(out[:, 384:512])]
+        return down_all([i])[0]
 
     ROWS4 = ((0, 208), (208, 416), (416, 624), (624, 656))
+
+    def store_units(*units):
+        for i, parts in zip(units, down_all(units)):
+            for (lo, hi), part in zip(ROWS4, parts):
+                PG[i, lo:hi] = part.astype(BF)
 
     def store_unit(i, *adds):
         for (lo, hi), part in zip(ROWS4, down(i)):
@@ -337,22 +348,20 @@
         rs(u, m, p, 0, buf, sib).wait_recv()
 
     def first_down(kk, carry):
-        k = 3 - kk
-        for u in UU:
-            i = uidx(u, da_of(k), 2)
-            store_unit(i)
-            rs(u, 3 + 3 * k, 0, i, rb1.at[u, k], bp[u]).start()
-            rs(u, 3 + 3 * k, 1, i, rb1.at[u, k], bm[u]).start()
+        ks = (3 - 2 * kk, 2 - 2 * kk)
+        store_units(*[uidx(u, da_of(k), 2) for k in ks for u in UU])
+        for k in ks:
+            for u in UU:
+                i = uidx(u, da_of(k), 2)
+                rs(u, 3 + 3 * k, 0, i, rb1.at[u, k], bp[u]).start()
+                rs(u, 3 + 3 * k, 1, i, rb1.at[u, k], bm[u]).start()
         return carry
 
     def second_free(k):
-        for u in UU:
-            i = uidx(u, da_of(k), 1)
-            store_unit(i)
-            rs(u, 4 + 3 * k, 1, i, rb2.at[u, 0, k], bp[u]).start()
-            i = uidx(u, da_of(k), 3)
-            store_unit(i)
-            rs(u, 5 + 3 * k, 0, i, rb2.at[u, 1, k], bm[u]).start()
+        store_units(*[uidx(u, da_of(k), db) for db in (1, 3) for u in UU])
+        for u in UU:
+            rs(u, 4 + 3 * k, 1, uidx(u, da_of(k), 1), rb2.at[u, 0, k], bp[u]).start()
+            rs(u, 5 + 3 * k, 0, uidx(u, da_of(k), 3), rb2.at[u, 1, k], bm[u]).start()
 
     def second_sum(k):
         for u in UU:
@@ -365,11 +374,6 @@
             add_part(i, 1, rb1.at[u, k])
             rs(u, 5 + 3 * k, 1, i, rb2.at[u, 1, k], bm[u]).start()
 
-    def second_down(kk, carry):
-        second_free(3 - kk)
-        second_sum(3 - kk)
-        return carry
-
     def third(u, k):
         for w in (0, 1):
             for p in (1, 0) if w == 0 else (0, 1):
@@ -382,19 +386,23 @@
         return lax.rem(z + r, 8)
 
     def mix(b):
-        def body(j, carry):
-            i = b * 4 + j
-            w = weight(i)
-            m = jnp.dot(w[96:208], ST[:, 256:512], preferred_element_type=F32)
-            row = lax.broadcasted_iota(jnp.int32, m.shape, 0)
+        def rows(lo):
+            tiles = []
+            for j in range(4):
+                w = [U[b * 4 + j, UR * t + lo : UR * t + lo + 112] for t in range(3)]
+                tiles.append(jnp.concatenate(w + [WT[b * 4 + j, lo : lo + 112]], axis=1))
+            return jnp.concatenate(tiles, axis=0)
+
+        ms = jnp.dot(rows(96), ST[:, 256:512], preferred_element_type=F32)
+        ns = jnp.dot(rows(0), ST[:, 0:256], preferred_element_type=F32).astype(BF)
+        row = lax.broadcasted_iota(jnp.int32, (112, 256), 0)
+        for j in range(4):
+            m = ms[112 * j : 112 * j + 112]
             m = jnp.where(row == 104, cen_hi, jnp.where(row == 105, cen_lo, m)).astype(BF)
-            n = jnp.dot(w[0:112], ST[:, 0:256], preferred_element_type=F32).astype(BF)
+            n = ns[112 * j : 112 * j + 112]
             for e in (0, 1):
-                M[e, 0, i] = m[:, 128 * e : 128 * e + 128]
-                M[e, 1, i] = n[:, 128 * e : 128 * e + 128]
-            return carry
-
-        lax.fori_loop(0, 4, body, 0)
+                M[e, 0, b * 4 + j] = m[:, 128 * e : 128 * e + 128]
+                M[e, 1, b * 4 + j] = n[:, 128 * e : 128 * e + 128]
 
     def to_sibling(s, r):
         b = 4 * zblk(r)
@@ -457,44 +465,38 @@
         return jnp.concatenate([v, jnp.zeros((16, 128), F32)], axis=0).T
 
     lax.fori_loop(0, 2, first_down, 0)
+    second_free(3)
     ST[...] = S[...].T
     center = cen[...].T[0:1]
     cen_hi = center.astype(BF).astype(F32)
     cen_lo = center - cen_hi
-    lax.fori_loop(0, 2, mix_step, 0)
-    lax.fori_loop(2, 4, first_down, 0)
-    lax.fori_loop(2, 4, mix_step, 0)
+    lax.fori_loop(0, 4, mix_step, 0)
     zfirst(0)
-    second_free(3)
+    second_free(2)
+    second_sum(3)
     lax.fori_loop(4, 8, mix_step, 0)
+    second_sum(2)
     zstep(0, 1)
     zfirst(1)
-    second_sum(3)
-    lax.fori_loop(1, 4, second_down, 0)
+    second_free(1)
+    second_sum(1)
+    second_free(0)
     zstep(0, 2)
+    second_sum(0)
     zstep(1, 1)
 
     for u in UU:
         i = third(u, 3)
         rs(u, 0, 0, i, ra1.at[u], ap[u]).start()
         rs(u, 0, 1, i, ra1.at[u], am[u]).start()
+    zstep(0, 3)
     for u in UU:
         i = third(u, 2)
         rs(u, 2, 0, i, ra2.at[u, 1], am[u]).start()
-    zstep(0, 3)
     zstep(1, 2)
     for u in UU:
         i = third(u, 1)
         rs(u, 1, 1, i, ra2.at[u, 0], ap[u]).start()
-    for u in UU:
-        rs_wait(u, 0, 0, ra1.at[u])
-        i = uidx(u, 1, 0)
-        add_part(i, 0, ra1.at[u])
-        rs(u, 1, 0, i, ra2.at[u, 0], ap[u]).start()
-        rs_wait(u, 0, 1, ra1.at[u])
-        i = uidx(u, 3, 0)
-        add_part(i, 1, ra1.at[u])
-        rs(u, 2, 1, i, ra2.at[u, 1], am[u]).start()
 
     to_sibling(7, 0).wait_recv()
     for h in (0, 1):
@@ -515,12 +517,18 @@
         if sh + FE > 128:
             wide[at + 1] = jnp.where(ln < sh + FE - 128, r, wide[at + 1])
     cen[0:128, :] = jnp.broadcast_to(centre, (128, 128))
-    tail = jnp.where(ln < 16, wide[3], 0.0)
+    to, fr = (lax.broadcasted_iota(jnp.int32, (128, 128), d) for d in (0, 1))
+    tr = lax.rem(to, 64)
+    perm = fr == 64 * (to // 64) + 32 * (tr // 32) + 2 * lax.rem(tr, 16) + lax.rem(tr // 16, 2)
+    wide = jnp.concatenate(wide, axis=1).astype(BF)
+    wide = jnp.dot(perm.astype(BF), wide, preferred_element_type=F32)
+    tail = jnp.where(ln < 16, wide[:, 384:512], 0.0)
+    wide = [wide[:, 128 * t : 128 * t + 128].astype(BF) for t in range(3)]
     folded = tail[0:16]
     for g in range(1, 8):
         folded = folded + pltpu.roll(tail[16 * g : 16 * g + 16], 16 * g, 1)
     for t in range(3):
-        V[c, me, 128 * t : 128 * t + 128, :] = wide[t].astype(BF)
+        V[c, me, 128 * t : 128 * t + 128, :] = wide[t]
     V[c, me, 384:400, :] = folded.astype(BF)
 
     VP = (((0, 112), (112, 96)), ((208, 96), (304, 96)))
@@ -541,6 +549,17 @@
         vg.start_b(u)
     for u in UU:
         fwd(u, 0, 0).start()
+
+    zstep(1, 3)
+    for u in UU:
+        rs_wait(u, 0, 0, ra1.at[u])
+        i = uidx(u, 1, 0)
+        add_part(i, 0, ra1.at[u])
+        rs(u, 1, 0, i, ra2.at[u, 0], ap[u]).start()
+        rs_wait(u, 0, 1, ra1.at[u])
+        i = uidx(u, 3, 0)
+        add_part(i, 1, ra1.at[u])
+        rs(u, 2, 1, i, ra2.at[u, 1], am[u]).start()
 
     def finish(u):
         for w in (0, 1):
@@ -558,31 +577,27 @@
             out.append(part)
         return i, out
 
-    zstep(1, 3)
+    for u in UU:
+        vg.near0(u)
+    for u in UU:
+        vg.near1(u)
+    for u in UU:
+        fwd(u, 3, 0).start()
+        fwd(u, 1, 0).start()
+    for u in UU:
+        vg.bfwd(u, 0)
     i, parts = finish(1)
     for (lo, hi), part in zip(ROWS4, parts):
         PG[i, lo:hi] = part.astype(BF)
     to_fin = rc(PG.at[i], fin, mi_s.at[2], mi_r.at[2], sib)
     to_fin.start()
     for u in UU:
-        vg.near0(u)
-    for u in UU:
-        vg.near1(u)
-    for u in UU:
-        fwd(u, 3, 0).start()
-        fwd(u, 1, 0).start()
-    for u in UU:
-        vg.bfwd(u, 0)
+        vg.far(u)
+        fwd(u, 2, 0).start()
     _, parts = finish(0)
     for t in range(3):
         GS[:, 128 * t : 128 * t + 128] = parts[t]
     GS[:, 384:512] = unfold_tail(parts[3])
-    for u in UU:
-        vg.far(u)
-        fwd(u, 2, 0).start()
-
-    hacc[...] = jnp.zeros_like(hacc)
-
     for h in (0, 1):
         for way in (0, 1):
             zcopy(1, way, 3, h).wait_recv()
@@ -596,12 +611,22 @@
         GP[FE * j : FE * j + FE, :] = gp.T[:FE]
     gp_out[...] = GP[...].astype(BF)
 
+    table = U[:, 192:208, :].astype(F32)[:, 8, :]
+    first_block = (dp * BLK).astype(F32)
+    hit = (table >= first_block) & (table < first_block + BLK)
+    hit = hit & (lax.broadcasted_iota(jnp.int32, table.shape, 1) < 2)
+    least = jnp.min(jnp.where(hit, table, 1000.0))
+    most = jnp.max(jnp.where(hit, table, -9.0))
+    to, fr = (lax.broadcasted_iota(jnp.int32, (128, 256), d) for d in (0, 1))
+    PM[...] = jnp.where(lax.rem(to, 64) == lax.rem(fr, 64), jnp.where(to < 64, least, most), -5.0)
+    hacc[0:128] = jnp.zeros((128, 512), F32)
+
     def take(ch):
         for u in UU:
             ref = V.at[1 - c, ch, pl.ds(208 * u, 208 - 16 * u)]
             rc(ref, ref, vf_s.at[u, ch], vf_r.at[u, ch], sib).wait_recv()
         rows = []
-        blocks = []
+        numbers = []
         ln = lax.broadcasted_iota(jnp.int32, (1, 128), 1)
         for e in (0, 1):
             tail = V[e, ch, 384:400].astype(F32)
@@ -611,9 +636,9 @@
                 jnp.concatenate([V[e, ch, 128 * t : 128 * t + 128] for t in range(3)] + [tail], axis=1)
             )
             pair = U[2 * ch + e, 192:208].astype(F32)[8:9]
-            blocks.append(jnp.where(ln < 64, pair[:, 0:1], pair[:, 1:2]))
-        place = (PM[...] == jnp.concatenate(blocks, axis=1)).astype(BF)
-        hacc[...] += jnp.dot(place, jnp.concatenate(rows, axis=0), preferred_element_type=F32)
+            numbers.append(jnp.where(ln < 64, pair[:, 0:1], pair[:, 1:2]))
+        place = (PM[...] == jnp.concatenate(numbers, axis=1)).astype(BF)
+        hacc[0:128] += jnp.dot(place, jnp.concatenate(rows, axis=0), preferred_element_type=F32)
 
     def take4(kind):
         def body(n, carry):
@@ -638,10 +663,7 @@
             fwd(u, da_of(k - 1), 1).start()
         return carry
 
-    take(me)
-    vstep(1, 0)
-    take4(0)
-    lax.fori_loop(2, 4, vstep, 0)
+    lax.fori_loop(1, 4, vstep, 0)
 
     to_fin.wait_recv()
     mine = GS[...]
@@ -652,11 +674,13 @@
         gin_out[:, HH * h : HH * h + HH] = half[0:FE, 0:HH]
         gout_out[:, HH * h : HH * h + HH] = half[FE : 2 * FE, 0:HH]
 
-    take4(1)
     for u in UU:
         vg.brest(u, 3)
         fwd(u, 2, 3).start()
         fwd(u, 2, 1).start()
+    take(me)
+    take4(0)
+    take4(1)
     for k in range(4):
         for u in UU:
             vg.blast(u, k)
@@ -664,11 +688,16 @@
         if k == 0:
             take(lax.rem(y, 4) * 4 + lax.rem(x + 2, 4))
             take(lax.rem(y + 2, 4) * 4 + x)
-        if k == 2:
-            take4(2)
+    take4(2)
     take(lax.rem(y + 2, 4) * 4 + lax.rem(x + 2, 4))
+    low, high = hacc[0:64], hacc[64:128]
+    for b in range(BLK):
+        number = first_block + float(b)
+        tile = jnp.where(least == number, low, jnp.where(most == number, high, 0.0)).astype(BF)
+        for q in range(4):
+            VT[q, 16 * b : 16 * b + 16, :] = tile[16 * q : 16 * q + 16]
     for q in range(4):
-        vis_out[q] = hacc[128 * q : 128 * q + 128, :].astype(BF).T[:HH]
+        vis_out[q] = VT[q].T[:HH]
 
     def vfwd_wait(ch, carry):
         for u in UU:
@@ -723,7 +752,8 @@
             pltpu.VMEM((2, 16, 3200), F32),
             pltpu.VMEM((128, 128), F32),
             pltpu.VMEM((2, 8, 3200), F32),
-            pltpu.VMEM((512, 256), F32),
+            pltpu.VMEM((128, 256), F32),
+            pltpu.VMEM((4, 128, 512), BF),
             pltpu.VMEM((UR, 896), F32),
             pltpu.VMEM((2, PK, 128), BF),
             pltpu.VMEM((2, 32, 8, 128), F32),

time: 105 us -> 96.7 us (0.921)
  Pallas kernels: 99.6 us -> 91.5 us
    pallas_call x1, Pallas kernels: 99.6 us -> 91.5 us  [mega(): pl.pallas_call(kernel, out_shape=(jax.ShapeDtypeStruct((FE, 2 * HH), F32)...]
where the time goes in v4:
time: 96.7 us; the launch traced here: 96.5 us
  Pallas kernels  91.5 us (95%)
  local copies, waits for them, and re-layouts  4.35 us (4%)
    pallas_call x1, Pallas kernels, mega(): pl.pallas_call(kernel, out_shape=(jax.ShapeDtypeStruct((FE, 2 * HH), F32)...  91.5 us
    unnamed x10, local copies, waits for them, and re-layouts  4.35 us

profile of v4, /device:TPU:1, one launch (start us, length us, event | category | flops | bytes accessed | tf_op | source)
XLA Modules:
  0.0 96.5 jit_solution(11674866621333166239)
XLA Ops:
  0.6 91.5 %shard_map.102 = (f32[100,800]{1,0:T(8,128)}, f32[100,800]{1,0:T(8,128)}, bf16[400,128]{1,0:T(8,128)(2,1)}, bf16[4,400,128]{2,1,0:T(8,128)(2,1)}) custom-call(s32[2]{0:T(128)} %slots.1, bf16[100,800]{1,0:T(8,128)(2,1)} %w_in.1, bf16[100,800]{1,0:T(8,128)(2,1)} %bitcast.8, f32[25,128]{1,0:T(8,128)} %bitcast.10, f32[25,128]{1,0:T(8,128)} %bitcast.11, ...), custom_call_target="tpu_custom_call" | custom-call | tf_op jit(solution)/shard_map/pallas_call | solution.py:738
  92.1 0.0 copy-start.2
  92.1 0.0 copy-start.1
  92.1 1.8 %copy.15 = bf16[128,4,400]{0,2,1:T(8,128)(2,1)} copy(bf16[128,4,400]{0,2,1:T(8,128)(2,1)} %bitcast.6) | data formatting | bytes 819200
  94.0 0.0 copy-done.2
  94.0 0.6 copy.16
  94.6 0.0 copy-done.1
  94.6 0.0 copy-start
  94.6 0.7 copy.17
  95.4 0.4 copy-done
  95.7 0.7 copy.18
Async XLA Ops:
  92.1 1.9 %copy-start.2 = (bf16[400,128]{1,0:T(8,128)(2,1)S(1)}, bf16[400,128]{1,0:T(8,128)(2,1)}, u32[]{:S(2)}) copy-start(bf16[400,128]{1,0:T(8,128)(2,1)} %get-tuple-element.9) | copy-start | bytes 307204
  92.1 2.5 %copy-start.1 = (f32[100,800]{1,0:T(8,128)S(1)}, f32[100,800]{1,0:T(8,128)}, u32[]{:S(2)}) copy-start(f32[100,800]{1,0:T(8,128)} %get-tuple-element.18) | copy-start | bytes 960004
  94.6 1.1 %copy-start = (f32[100,800]{1,0:T(8,128)S(1)}, f32[100,800]{1,0:T(8,128)}, u32[]{:S(2)}) copy-start(f32[100,800]{1,0:T(8,128)} %get-tuple-element.11) | copy-start | bytes 960004

commit v5 on v4

--- a/solution.py
+++ b/solution.py
@@ -32,8 +32,8 @@
 
 
 def kernel(
-    slots, w_in, w_out, gain, lscale, patches, upstream, gin_out, gout_out, gp_out, vis_out,
-    xin, uin, nsc, rsc, RM, VC, PM, VT, WB, wu, GU, U, WT, C2, XU, XP, CT, hacc, S, ST, PG, rb1, rb2, ra1, ra2, fin, GS,
+    slots, w_in_hbm, w_out_hbm, gain_hbm, lscale_hbm, patches, upstream, gin_out, gout_out, gp_out, vis_out,
+    gin_v, gout_v, gp_v, vis, w_in, w_out, gain, lscale, xin, uin, nsc, rsc, RM, VC, PM, VT, WB, wu, GU, U, WT, C2, XU, XP, CT, hacc, S, ST, PG, rb1, rb2, ra1, ra2, fin, GS,
     M, MR, zrm, zrp, V, GP, cen,
     ag_s, ag_r, rs_s, rs_r, vg_s, vg_r, vf_s, vf_r, sq_s, sq_r, zz_s, zz_r, mi_s, mi_r, loc,
 ):
@@ -76,12 +76,22 @@
 
     get_p = pltpu.make_async_copy(patches, xin, loc.at[1])
     get_u = pltpu.make_async_copy(upstream, uin, loc.at[2])
+    small = [
+        pltpu.make_async_copy(a, b, loc.at[3 + n])
+        for n, (a, b) in enumerate(
+            ((w_in_hbm, w_in), (w_out_hbm, w_out), (gain_hbm, gain), (lscale_hbm, lscale))
+        )
+    ]
+    for copy in small:
+        copy.start()
     get_p.start()
     get_u.start()
     barrier = pltpu.get_barrier_semaphore()
     for d in nbrs:
         pl.semaphore_signal(barrier, inc=1, device_id=d, device_id_type=MESH)
 
+    for copy in small:
+        copy.wait()
     WB[0:FE, 0:800] = w_in[...].astype(F32)
     WB[FE : 2 * FE, 0:800] = w_out[...].astype(F32)
     at = lax.broadcasted_iota(jnp.int32, (8, 800), 1)
@@ -609,7 +619,7 @@
         moved = pltpu.roll(XP[i].astype(F32), 124, 1)
         gp = XU[i].astype(F32) + (GU[0, i][0:1] * t - moved / root * centre) / root
         GP[FE * j : FE * j + FE, :] = gp.T[:FE]
-    gp_out[...] = GP[...].astype(BF)
+    gp_v[...] = GP[...].astype(BF)
 
     table = U[:, 192:208, :].astype(F32)[:, 8, :]
     first_block = (dp * BLK).astype(F32)
@@ -671,8 +681,35 @@
     other = jnp.concatenate(other, axis=1)
     for h in (0, 1):
         half = jnp.where(c == h, mine, other)
-        gin_out[:, HH * h : HH * h + HH] = half[0:FE, 0:HH]
-        gout_out[:, HH * h : HH * h + HH] = half[FE : 2 * FE, 0:HH]
+        gin_v[:, HH * h : HH * h + HH] = half[0:FE, 0:HH]
+        gout_v[:, HH * h : HH * h + HH] = half[FE : 2 * FE, 0:HH]
+    outs = [
+        pltpu.make_async_copy(a, b, loc.at[3 + n])
+        for n, (a, b) in enumerate(((gin_v, gin_out), (gout_v, gout_out), (gp_v, gp_out)))
+    ]
+    for copy in outs:
+        copy.start()
+
+    ag.done()
+    to_sib.wait_send()
+    act_sib.wait_send()
+    for n in range(8):
+        to_sibling(n, zorder[n]).wait_send()
+    for t in (0, 1):
+        for way in (0, 1):
+            zcopy(t, way, 0, way).wait_send()
+            for n in (1, 2, 3):
+                for h in (0, 1):
+                    zcopy(t, way, n, h).wait_send()
+
+    def rs_done(m, carry):
+        for u in UU:
+            for p in (0, 1):
+                rs(u, m, p, 0, ra1.at[u], sib).wait_send()
+        return carry
+
+    lax.fori_loop(0, 15, rs_done, 0)
+    to_fin.wait_send()
 
     for u in UU:
         vg.brest(u, 3)
@@ -697,7 +734,7 @@
         for q in range(4):
             VT[q, 16 * b : 16 * b + 16, :] = tile[16 * q : 16 * q + 16]
     for q in range(4):
-        vis_out[q] = VT[q].T[:HH]
+        vis[q] = VT[q].T[:HH]
 
     def vfwd_wait(ch, carry):
         for u in UU:
@@ -707,32 +744,16 @@
 
     lax.fori_loop(0, 16, vfwd_wait, 0)
 
-    ag.done()
     vg.done()
-    to_sib.wait_send()
-    act_sib.wait_send()
-    to_fin.wait_send()
-    for s in range(8):
-        to_sibling(s, zorder[s]).wait_send()
-    for t in (0, 1):
-        for way in (0, 1):
-            zcopy(t, way, 0, way).wait_send()
-            for j in (1, 2, 3):
-                for h in (0, 1):
-                    zcopy(t, way, j, h).wait_send()
-
-    def rs_done(m, carry):
-        for u in UU:
-            for p in (0, 1):
-                rs(u, m, p, 0, ra1.at[u], sib).wait_send()
-        return carry
-
-    lax.fori_loop(0, 15, rs_done, 0)
+    for copy in outs:
+        copy.wait()
+    last = pltpu.make_async_copy(vis, vis_out, loc.at[2])
+    last.start()
+    last.wait()
 
 
 def mega(slots, w_in, w_out, gain, lscale, patches, upstream):
     dma = pltpu.SemaphoreType.DMA
-    vm = pl.BlockSpec(memory_space=pltpu.VMEM)
     sm = pl.BlockSpec(memory_space=pltpu.SMEM)
     hbm = pl.BlockSpec(memory_space=pl.ANY)
     return pl.pallas_call(
@@ -743,9 +764,17 @@
             jax.ShapeDtypeStruct((HH, 128), BF),
             jax.ShapeDtypeStruct((4, HH, BLK * 16), BF),
         ),
-        in_specs=[sm, vm, vm, vm, vm, hbm, hbm],
-        out_specs=(vm, vm, vm, vm),
+        in_specs=[sm, hbm, hbm, hbm, hbm, hbm, hbm],
+        out_specs=(hbm, hbm, hbm, hbm),
         scratch_shapes=[
+            pltpu.VMEM((FE, 2 * HH), F32),
+            pltpu.VMEM((FE, 2 * HH), F32),
+            pltpu.VMEM((HH, 128), BF),
+            pltpu.VMEM((4, HH, BLK * 16), BF),
+            pltpu.VMEM((FE, 2 * HH), BF),
+            pltpu.VMEM((FE, 2 * HH), BF),
+            pltpu.VMEM((25, 128), F32),
+            pltpu.VMEM((25, 128), F32),
             pltpu.VMEM((128, 3200), BF),
             pltpu.VMEM((128, 3200), BF),
             pltpu.VMEM((2, 16, 3200), F32),
@@ -787,7 +816,7 @@
             dma((8,)), dma((8,)),
             dma((2, 2, 4, 2)), dma((2, 2, 4, 2)),
             dma((3,)), dma((3,)),
-            dma((3,)),
+            dma((7,)),
         ],
         compiler_params=pltpu.CompilerParams(
             collective_id=0, has_side_effects=True, vmem_limit_bytes=60 * 2**20

time: 96.7 us -> 95.7 us (0.990)
  Pallas kernels: 91.5 us -> 90.5 us
    pallas_call x1, Pallas kernels: 91.5 us -> 90.5 us  [mega(): pl.pallas_call(kernel, out_shape=(jax.ShapeDtypeStruct((FE, 2 * HH), F32)...]
where the time goes in v5:
time: 95.7 us; the launch traced here: 95.5 us
  Pallas kernels  90.5 us (95%)
  local copies, waits for them, and re-layouts  4.35 us (5%)
    pallas_call x1, Pallas kernels, mega(): pl.pallas_call(kernel, out_shape=(jax.ShapeDtypeStruct((FE, 2 * HH), F32)...  90.5 us
    unnamed x10, local copies, waits for them, and re-layouts  4.35 us

profile of v5, /device:TPU:1, one launch (start us, length us, event | category | flops | bytes accessed | tf_op | source)
XLA Modules:
  0.0 95.5 jit_solution(6563626728066530429)
XLA Ops:
  0.6 90.5 %shard_map.102 = (f32[100,800]{1,0:T(8,128)}, f32[100,800]{1,0:T(8,128)}, bf16[400,128]{1,0:T(8,128)(2,1)}, bf16[4,400,128]{2,1,0:T(8,128)(2,1)}) custom-call(s32[2]{0:T(128)} %slots.1, bf16[100,800]{1,0:T(8,128)(2,1)} %w_in_hbm.1, bf16[100,800]{1,0:T(8,128)(2,1)} %bitcast.8, f32[25,128]{1,0:T(8,128)} %bitcast.10, f32[25,128]{1,0:T(8,128)} %bitcast.11, ...), custom_call_target="tpu_custom_call" | custom-call | tf_op jit(solution)/shard_map/pallas_call | solution.py:759
  91.1 0.0 copy-start.2
  91.1 0.0 copy-start.1
  91.1 1.8 %copy.15 = bf16[128,4,400]{0,2,1:T(8,128)(2,1)} copy(bf16[128,4,400]{0,2,1:T(8,128)(2,1)} %bitcast.6) | data formatting | bytes 819200
  93.0 0.0 copy-done.2
  93.0 0.6 copy.16
  93.6 0.0 copy-done.1
  93.6 0.0 copy-start
  93.6 0.7 copy.17
  94.4 0.4 copy-done
  94.7 0.7 copy.18
Async XLA Ops:
  91.1 1.9 %copy-start.2 = (bf16[400,128]{1,0:T(8,128)(2,1)S(1)}, bf16[400,128]{1,0:T(8,128)(2,1)}, u32[]{:S(2)}) copy-start(bf16[400,128]{1,0:T(8,128)(2,1)} %get-tuple-element.9) | copy-start | bytes 307204
  91.1 2.5 %copy-start.1 = (f32[100,800]{1,0:T(8,128)S(1)}, f32[100,800]{1,0:T(8,128)}, u32[]{:S(2)}) copy-start(f32[100,800]{1,0:T(8,128)} %get-tuple-element.18) | copy-start | bytes 960004
  93.6 1.1 %copy-start = (f32[100,800]{1,0:T(8,128)S(1)}, f32[100,800]{1,0:T(8,128)}, u32[]{:S(2)}) copy-start(f32[100,800]{1,0:T(8,128)} %get-tuple-element.11) | copy-start | bytes 960004

commit v6 on v5

--- a/solution.py
+++ b/solution.py
@@ -61,7 +61,8 @@
     am = [dev(u, 3, 0) for u in UU]
     bp = [dev(u, 0, 1) for u in UU]
     bm = [dev(u, 0, 3) for u in UU]
-    nbrs = [sib, ap[0], am[0], bp[0], bm[0], zdev(1), zdev(7)]
+    cross = [(chip_of(1, da, db) * 2 + 1 - c, z) for da, db in ((1, 0), (3, 0), (0, 1), (0, 3))]
+    nbrs = [sib, ap[0], am[0], bp[0], bm[0], zdev(1), zdev(7)] + cross
 
     def rc(src, dst, ss, rs, d):
         return pltpu.make_async_remote_copy(
@@ -197,9 +198,11 @@
     own.start()
     ag.start_a(0, wu)
     ag.start_b(0, wu)
-    rc(wu.at[0], U.at[me * 2 + 1 - c], mi_s.at[0], mi_r.at[0], sib).wait_recv()
-    ag.start_a(1)
-    ag.start_b(1)
+    for m, p, n in ((0, 0, 0), (1, 1, 1), (0, 1, 0), (1, 0, 1), (3, 0, 2), (4, 1, 3), (3, 1, 2), (4, 0, 3)):
+        part = pl.ds(*PARTS[p])
+        rc(
+            wu.at[1 - c, part], U.at[me * 2 + c, part], ag_s.at[1, m, p], ag_r.at[1, m, p], cross[n]
+        ).start()
 
     hacc[...] = jnp.zeros_like(hacc)
     get_p.wait()
@@ -269,6 +272,7 @@
     for u in UU:
         ag.bfwd(u, 0)
     own.wait()
+    rc(wu.at[0], U.at[me * 2 + 1 - c], mi_s.at[0], mi_r.at[0], sib).wait_recv()
     up_all([(0, 0, 0), (1, 0, 0)])
     for u in UU:
         ag.far(u)

time: 95.7 us -> 95.7 us (level)
  no operation moved by 1% of the time
where the time goes in v6:
time: 95.7 us; the launch traced here: 95.5 us
  Pallas kernels  90.5 us (95%)
  local copies, waits for them, and re-layouts  4.35 us (5%)
    pallas_call x1, Pallas kernels, mega(): pl.pallas_call(kernel, out_shape=(jax.ShapeDtypeStruct((FE, 2 * HH), F32)...  90.5 us
    unnamed x10, local copies, waits for them, and re-layouts  4.35 us

profile of v6, /device:TPU:1, one launch (start us, length us, event | category | flops | bytes accessed | tf_op | source)
XLA Modules:
  0.0 95.5 jit_solution(14946827834609176766)
XLA Ops:
  0.6 90.5 %shard_map.102 = (f32[100,800]{1,0:T(8,128)}, f32[100,800]{1,0:T(8,128)}, bf16[400,128]{1,0:T(8,128)(2,1)}, bf16[4,400,128]{2,1,0:T(8,128)(2,1)}) custom-call(s32[2]{0:T(128)} %slots.1, bf16[100,800]{1,0:T(8,128)(2,1)} %w_in_hbm.1, bf16[100,800]{1,0:T(8,128)(2,1)} %bitcast.8, f32[25,128]{1,0:T(8,128)} %bitcast.10, f32[25,128]{1,0:T(8,128)} %bitcast.11, ...), custom_call_target="tpu_custom_call" | custom-call | tf_op jit(solution)/shard_map/pallas_call | solution.py:763
  91.2 0.0 copy-start.2
  91.2 0.0 copy-start.1
  91.2 1.8 %copy.15 = bf16[128,4,400]{0,2,1:T(8,128)(2,1)} copy(bf16[128,4,400]{0,2,1:T(8,128)(2,1)} %bitcast.6) | data formatting | bytes 819200
  93.0 0.0 copy-done.2
  93.0 0.6 copy.16
  93.7 0.0 copy-done.1
  93.7 0.0 copy-start
  93.7 0.7 copy.17
  94.4 0.4 copy-done
  94.8 0.7 copy.18
Async XLA Ops:
  91.2 1.9 %copy-start.2 = (bf16[400,128]{1,0:T(8,128)(2,1)S(1)}, bf16[400,128]{1,0:T(8,128)(2,1)}, u32[]{:S(2)}) copy-start(bf16[400,128]{1,0:T(8,128)(2,1)} %get-tuple-element.9) | copy-start | bytes 307204
  91.2 2.5 %copy-start.1 = (f32[100,800]{1,0:T(8,128)S(1)}, f32[100,800]{1,0:T(8,128)}, u32[]{:S(2)}) copy-start(f32[100,800]{1,0:T(8,128)} %get-tuple-element.18) | copy-start | bytes 960004
  93.7 1.1 %copy-start = (f32[100,800]{1,0:T(8,128)S(1)}, f32[100,800]{1,0:T(8,128)}, u32[]{:S(2)}) copy-start(f32[100,800]{1,0:T(8,128)} %get-tuple-element.11) | copy-start | bytes 960004
